TPU v7x, 128 devices: a whole 4x4x4 slice. The times are simulated.
128 devices in a mesh: dp: 4 (over y), expert: 32 (over x, z, core).
Axes of the slice: x: 4, y: 4, z: 4, core: 2. Of those that a mesh axis runs over, the one named last changes fastest.
Arguments:
- tokens: bfloat16 [16384, 2560], P(('dp', 'expert')), may hold values from -6 to 6
- cotangent: bfloat16 [16384, 2560], P(('dp', 'expert')), may hold values from -4 to 4
- expert_ids: int32 [16384, 6], P(('dp', 'expert')), may hold values from 0 to 31, all different within a row; in each aligned block of 128 rows (0 to 127, 128 to 255, ...) at most 48 rows name the same one
- router_probs: float32 [16384, 6], P(('dp', 'expert')), may hold values from 0.05 to 1
- spare_replica: int32 [32, 4], P('expert'), may hold values from 0 to 3, as said below
- w_gate: bfloat16 [32, 2560, 832], P('expert'), may hold values from -0.125 to 0.125
- w_up: bfloat16 [32, 2560, 832], P('expert'), may hold values from -0.125 to 0.125
- w_down: bfloat16 [32, 832, 2560], P('expert'), may hold values from -0.21875 to 0.21875
Outputs:
- token_grad: bfloat16 [16384, 2560], P(('dp', 'expert'))
- prob_grad: float32 [16384, 6], P(('dp', 'expert'))
- grad_gate: bfloat16 [32, 2560, 832], P('expert', 'dp')
- grad_up: bfloat16 [32, 2560, 832], P('expert', 'dp')
- grad_down: bfloat16 [32, 832, 2560], P('expert', 'dp')
Inputs may be any that keep to these rules, and one draw needn't show every extreme that they name: `expert_ids`: each token names 6 different experts. Among the 128 tokens of one device no expert is named by more than 48 tokens, and in every draw some device has an expert named by exactly 48 of its tokens. spare_replica[e, r] == r means that dp row r has no spare replica for expert e.
All inputs are finite; a program needn't handle non-finite values.
Results may differ from a plain program's by a relative error of at most 0.014.
Values may be sent and summed in bfloat16 or wider, within the bound.
No kernel may reach another device: no remote copies, remote signals or barrier semaphores. Data moves between devices by JAX's collectives and lax.ppermute only.
A program may use at most 192 MiB of HBM per device.

v0:
```python
import functools

import jax
import jax.numpy as jnp
from jax import lax
from jax.experimental import pallas as pl
from jax.experimental.pallas import tpu as pltpu
from jax.sharding import PartitionSpec as P

BF = jnp.bfloat16
F32 = jnp.float32
N_REP = 4
N_EXP = 32


def along_y(v, by):
    return lax.ppermute(v, "dp", [(r, (r + by) % N_REP) for r in range(N_REP)])


VMEM_LIMIT = 56 * 1024 * 1024


def join_wide_kernel(near_ref, far_ref, low_ref, high_ref, dep_ref, ahead_ref, behind_ref):
    half = low_ref.shape[1]
    ahead_ref[:, :half] = (near_ref[:, :half].astype(F32) + low_ref[...].astype(F32)).astype(BF)
    ahead_ref[:, half:] = near_ref[:, half:]
    behind_ref[:, :half] = far_ref[:, :half]
    behind_ref[:, half:] = (far_ref[:, half:].astype(F32) + high_ref[...].astype(F32)).astype(BF)


def join_pair_kernel(
    near_a, near_b, far_a, far_b, low_ref, high_ref, dep_ref, ahead_ref, behind_ref
):
    half = low_ref.shape[0]
    ahead_ref[:half] = (near_a[...].astype(F32) + low_ref[...].astype(F32)).astype(BF)
    ahead_ref[half:] = near_b[...]
    behind_ref[:half] = far_a[...]
    behind_ref[half:] = (far_b[...].astype(F32) + high_ref[...].astype(F32)).astype(BF)


def join(kernel, shape, arrays, dep):
    return pl.pallas_call(
        kernel,
        in_specs=[pl.BlockSpec(memory_space=pltpu.VMEM)] * len(arrays)
        + [pl.BlockSpec(memory_space=pl.ANY)],
        out_specs=[pl.BlockSpec(memory_space=pltpu.VMEM)] * 2,
        out_shape=[jax.ShapeDtypeStruct(shape, BF)] * 2,
        compiler_params=pltpu.CompilerParams(vmem_limit_bytes=VMEM_LIMIT),
        cost_estimate=pl.CostEstimate(flops=1000, bytes_accessed=1000, transcendentals=0),
    )(*arrays, dep)


def pick_kernel(most, tile, base_ref, slot_ref, rows_ref, out_ref, acc):
    group = pl.program_id(0)
    slots, width = out_ref.shape

    @pl.when(group == 0)
    def _():
        acc[...] = jnp.zeros_like(acc)

    base = pl.multiple_of(base_ref[group], 16)
    iota = lax.broadcasted_iota(jnp.int32, (most, rows_ref.shape[0]), 0) + base
    hot = (iota == slot_ref[...]).astype(BF)
    at = pl.ds(base, most)
    for w in range(0, width, tile):
        part = jnp.dot(hot, rows_ref[:, w : w + tile], preferred_element_type=F32)
        acc[at, w : w + tile] = acc[at, w : w + tile] + part.astype(BF)

    @pl.when(group == pl.num_programs(0) - 1)
    def _():
        out_ref[...] = acc[:slots, :]


def pick(rows, slot, first, slots, most_block, blocks):
    tokens, width = rows.shape
    count = tokens // first.shape[0]
    groups = first.shape[0] // blocks
    most = blocks * most_block + 16
    base = jnp.minimum(first.reshape(groups, blocks)[:, 0], slots) // 16 * 16
    return pl.pallas_call(
        functools.partial(pick_kernel, most, min(512, width)),
        grid_spec=pltpu.PrefetchScalarGridSpec(
            num_scalar_prefetch=1,
            grid=(groups,),
            in_specs=[
                pl.BlockSpec((None, 1, blocks * count), lambda g, base: (g, 0, 0)),
                pl.BlockSpec((blocks * count, width), lambda g, base: (g, 0)),
            ],
            out_specs=pl.BlockSpec((slots, width), lambda g, base: (0, 0)),
            scratch_shapes=[pltpu.VMEM((slots + most, width), BF)],
        ),
        out_shape=jax.ShapeDtypeStruct((slots, width), BF),
        compiler_params=pltpu.CompilerParams(vmem_limit_bytes=VMEM_LIMIT),
        cost_estimate=pl.CostEstimate(
            flops=2 * most * tokens * width,
            bytes_accessed=2 * width * (tokens + slots),
            transcendentals=0,
        ),
    )(base, slot.reshape(groups, 1, blocks * count), rows)


def pack_kernel(most_block, tile, first_ref, base_ref, row_ref, rows_ref, out_ref, acc):
    group = pl.program_id(0)
    slots, width = rows_ref.shape
    most = row_ref.shape[0] + 16

    @pl.when(group == 0)
    def _():
        acc[:slots, :] = rows_ref[...]
        acc[slots:, :] = jnp.zeros((acc.shape[0] - slots, width), BF)

    base = pl.multiple_of(base_ref[group], 16)
    iota = lax.broadcasted_iota(jnp.int32, (row_ref.shape[0], most), 1) + base
    hot = (iota == row_ref[...]).astype(BF)
    at = pl.ds(base, most)
    for w in range(0, width, tile):
        out_ref[:, w : w + tile] = jnp.dot(
            hot, acc[at, w : w + tile], preferred_element_type=F32
        ).astype(BF)


def pack(rows, first, most_block, blocks):
    slots, width = rows.shape
    groups = first.shape[0] // blocks
    first = jnp.minimum(first, slots)
    base = first.reshape(groups, blocks)[:, 0] // 16 * 16
    wanted = (first[:, None] + jnp.arange(most_block, dtype=jnp.int32)[None, :]).reshape(-1, 1)
    per = blocks * most_block
    return pl.pallas_call(
        functools.partial(pack_kernel, most_block, min(512, width)),
        grid_spec=pltpu.PrefetchScalarGridSpec(
            num_scalar_prefetch=2,
            grid=(groups,),
            in_specs=[
                pl.BlockSpec((per, 1), lambda g, *_: (g, 0)),
                pl.BlockSpec((slots, width), lambda g, *_: (0, 0)),
            ],
            out_specs=pl.BlockSpec((per, width), lambda g, *_: (g, 0)),
            scratch_shapes=[pltpu.VMEM((slots + per + 16, width), BF)],
        ),
        out_shape=jax.ShapeDtypeStruct((groups * per, width), BF),
        compiler_params=pltpu.CompilerParams(vmem_limit_bytes=VMEM_LIMIT),
        cost_estimate=pl.CostEstimate(
            flops=2 * groups * per * (per + 16) * width,
            bytes_accessed=2 * width * (slots + groups * per),
            transcendentals=0,
        ),
    )(first, base, wanted, rows)


def one_hot(slot, slots):
    return (lax.broadcasted_iota(jnp.int32, (slots, slot.shape[0]), 0) == slot[None, :]).astype(BF)


def placement(weight, spares, rep, cap, spare_cap):
    named = weight > 0
    load = jnp.sum(named.astype(jnp.int32))
    load = lax.all_gather(jnp.broadcast_to(load, (1, 128)), "dp", axis=0, tiled=True)[:, 0]
    excess = jnp.maximum(load - cap, 0)
    iota = jnp.arange(N_REP, dtype=jnp.int32)
    same = spares == spares[rep]
    offset = jnp.sum(jnp.where(same & (iota < rep) & (spares != iota), excess, 0))
    extra = jnp.where(spares[rep] != rep, jnp.maximum(spare_cap - offset, 0), 0)
    running, totals = running_count(named)
    before = jnp.cumsum(totals) - totals
    position = before[:, None] + running - 1
    placed = named & (position < cap + extra)
    return jnp.where(placed, position, -1), before


def running_count(named):
    count = named.shape[-1]
    upto = (
        lax.broadcasted_iota(jnp.int32, (count, count), 0)
        <= lax.broadcasted_iota(jnp.int32, (count, count), 1)
    ).astype(BF)
    running = jnp.dot(named.astype(BF), upto, preferred_element_type=F32).astype(jnp.int32)
    return running, running[:, -1]


def local(tokens, cotangent, expert_ids, router_probs, spare_replica, w_gate, w_up, w_down):
    rep = lax.axis_index("dp")
    count, width = tokens.shape
    top = expert_ids.shape[1]
    cap = count * top
    spare_cap = cap // 8
    slots = cap + spare_cap
    gate, upper, lower = w_gate[0], w_up[0], w_down[0]
    ff = gate.shape[1]
    total = jnp.sum(router_probs, axis=1, keepdims=True)
    scale = router_probs / total
    scale_b = scale.astype(BF)

    named_here = expert_ids.T[None] == jnp.arange(N_EXP, dtype=jnp.int32)[:, None, None]
    weight = jnp.sum(jnp.where(named_here, scale_b.T.astype(F32)[None], 0.0), axis=1).astype(BF)
    weight = lax.all_to_all(weight, "expert", split_axis=0, concat_axis=0, tiled=True)

    x_all = lax.all_gather(tokens, "expert", axis=0, tiled=True)
    dy_all = lax.all_gather(cotangent, "expert", axis=0, tiled=True)

    slot, first = placement(weight, spare_replica[0], rep, cap, spare_cap)

    chosen = one_hot(slot.reshape(-1), slots)
    row_scale = jnp.dot(chosen, weight.reshape(-1, 1), preferred_element_type=F32)
    most_block = min(count, 2 * count * top // N_EXP)
    rows_in = pick(x_all, slot.reshape(-1), first, slots, most_block, 4)
    hidden = jnp.dot(rows_in, gate, preferred_element_type=F32)
    lifted = jnp.dot(rows_in, upper, preferred_element_type=F32)
    logistic = jax.nn.sigmoid(hidden)
    swished = hidden * logistic
    activated = (swished * lifted).astype(BF)
    cot_rows = pick(dy_all, slot.reshape(-1), first, slots, most_block, 4)
    grad_out = (row_scale * cot_rows.astype(F32)).astype(BF)
    part_lower = lax.dot_general(
        activated, grad_out, (((0,), (0,)), ((), ())), preferred_element_type=F32
    ).astype(BF)
    rows_l, half_w = ff // N_REP, width // 2
    lower_term = [
        lax.dynamic_slice_in_dim(part_lower, ((rep + d) % N_REP) * rows_l, rows_l, 0)
        for d in range(N_REP)
    ]
    lower_low = along_y(lower_term[2][:, :half_w], 1)
    lower_high = along_y(lower_term[2][:, half_w:], -1)

    pulled = lax.dot_general(
        cot_rows, lower, (((1,), (1,)), ((), ())), preferred_element_type=F32
    )
    shares = jnp.sum(activated.astype(F32) * pulled, axis=1).astype(BF)
    grad_act = row_scale * pulled
    grad_hidden = (grad_act * lifted * logistic * (1.0 + hidden * (1.0 - logistic))).astype(BF)
    grad_lifted = (grad_act * swished).astype(BF)

    cut = width // N_REP
    columns = [
        lax.dynamic_slice_in_dim(rows_in, ((rep + d) % N_REP) * cut, cut, 1) for d in range(N_REP)
    ]

    def weight_term(grad, d):
        return lax.dot_general(
            grad, columns[d], (((0,), (0,)), ((), ())), preferred_element_type=F32
        ).astype(BF)

    gate_low = along_y(weight_term(grad_hidden, 2), 1)
    upper_high = along_y(weight_term(grad_lifted, 2), -1)

    back = lax.dot_general(grad_hidden, gate, (((1,), (1,)), ((), ())), preferred_element_type=F32)
    back = back + lax.dot_general(
        grad_lifted, upper, (((1,), (1,)), ((), ())), preferred_element_type=F32
    )
    back = back.astype(BF)
    packed = pack(back, first, most_block, 4).reshape(N_EXP, most_block, width)
    came = lax.all_to_all(packed, "expert", split_axis=0, concat_axis=0, tiled=True)

    ahead_l, behind_l = join(
        join_wide_kernel,
        (rows_l, width),
        (lower_term[1], lower_term[3], lower_low, lower_high),
        packed,
    )
    lower_got = along_y(ahead_l, 1), along_y(behind_l, -1)
    ahead, behind = join(
        join_pair_kernel,
        (2 * ff, cut),
        [weight_term(g, d) for d in (1, 3) for g in (grad_hidden, grad_lifted)]
        + [gate_low, upper_high],
        ahead_l,
    )
    weight_got = along_y(ahead, 1), along_y(behind, -1)
    named_any = jnp.any(named_here, axis=1)
    rank = jnp.where(named_any, running_count(named_any)[0] - 1, -1)
    hot = rank.T[:, :, None] == jnp.arange(most_block, dtype=jnp.int32)[None, None, :]
    token_grad = jnp.dot(
        hot.reshape(count, -1).astype(BF), came.reshape(-1, width), preferred_element_type=F32
    ).astype(BF)

    grad_lower = lower_term[0].astype(F32) + lower_got[0].astype(F32) + lower_got[1].astype(F32)
    grad_gate, grad_upper = [
        weight_term(g, 0).astype(F32) + sum(v[at : at + ff].astype(F32) for v in weight_got)
        for g, at in ((grad_hidden, 0), (grad_lifted, ff))
    ]

    share_rows = jnp.sum(
        jnp.where(
            lax.broadcasted_iota(jnp.int32, (N_EXP * count, slots), 1) == slot.reshape(-1)[:, None],
            shares.astype(F32)[None, :],
            0.0,
        ),
        axis=1,
    ).astype(BF)
    share_all = lax.all_to_all(
        share_rows.reshape(N_EXP, count), "expert", split_axis=0, concat_axis=0, tiled=True
    )
    mine = expert_ids[:, :, None] == jnp.arange(N_EXP, dtype=jnp.int32)[None, None, :]
    share = jnp.sum(jnp.where(mine, share_all.T.astype(F32)[:, None, :], 0.0), axis=2)
    prob_grad = (share - jnp.sum(scale * share, axis=1, keepdims=True)) / total

    return (
        token_grad,
        prob_grad,
        grad_gate.astype(BF).T[None],
        grad_upper.astype(BF).T[None],
        grad_lower.astype(BF)[None],
    )


def solution(mesh):
    return jax.shard_map(
        local,
        mesh=mesh,
        in_specs=(
            P(("dp", "expert"), None),
            P(("dp", "expert"), None),
            P(("dp", "expert"), None),
            P(("dp", "expert"), None),
            P("expert", None),
            P("expert", None, None),
            P("expert", None, None),
            P("expert", None, None),
        ),
        out_specs=(
            P(("dp", "expert"), None),
            P(("dp", "expert"), None),
            P("expert", "dp", None),
            P("expert", "dp", None),
            P("expert", "dp", None),
        ),
        check_vma=False,
    )
```

profile of v0, /device:TPU:32, one launch (start us, length us, event | category | flops | bytes accessed | tf_op | source)
XLA Modules:
  0.0 403.2 jit_solution(9146549915456125862)
XLA Ops:
  11.4 8.0 %all-to-all-start = ((bf16[32,1,128]{2,1,0:T(2,128)(2,1)}), bf16[32,1,128]{2,1,0:T(2,128)(2,1)S(1)}, u32[]{:S(2)}, u32[]{:S(2)}) async-start(bf16[32,1,128]{2,1,0:T(2,128)(2,1)} %copy.28), calls=%async_computation | async-start | bytes 32768 | tf_op jit(solution)/shard_map/all_to_all | solution.py:196
  21.9 3.6 all-to-all-done
  28.2 9.1 %all-reduce = s32[4]{0:T(128)S(1)} all-reduce(s32[4]{0:T(128)S(1)} %dynamic-update-slice), channel_id=2, replica_groups=mesh['dp'=4,'expert'=32] {'dp'}, use_global_device_ids=true, to_apply=%add | all-reduce | flops 4 | bytes 32
  45.6 48.5 %all-gather.5.cloned.1.call-done.rows_ref = bf16[4096,2560]{1,0:T(8,128)(2,1)} async-done(((bf16[128,2560]{1,0:T(8,128)(2,1)}), bf16[4096,2560]{1,0:T(8,128)(2,1)}) %all-gather.5.cloned.1.call-update) | async-done | bytes 20971536 | tf_op jit(solution)/shard_map/all_gather | solution.py:198
  94.1 15.0 %shard_map.120 = bf16[864,2560]{1,0:T(8,128)(2,1)} custom-call(s32[8]{0:T(128)} %fusion.45.base_ref, s32[8,1,512]{2,1,0:T(1,128)} %bitcast.86, bf16[4096,2560]{1,0:T(8,128)(2,1)} %all-gather.5.cloned.1.call-done.rows_ref), custom_call_target="tpu_custom_call" | custom-call | flops 4362076160 | bytes 25395200 | tf_op jit(solution)/shard_map/pallas_call | solution.py:80
  109.1 10.0 %fusion.5 = f32[864,832]{0,1:T(8,128)} fusion(bf16[864,2560]{1,0:T(8,128)(2,1)} %shard_map.120, bf16[1,2560,832]{1,2,0:T(8,128)(2,1)} %param.13), kind=kOutput, calls=%fused_computation.11 | convolution fusion | flops 3680501760 | bytes 11558912 | tf_op jit(solution)/shard_map/dot_general | solution.py:207
  119.1 6.2 %fusion.8 = f32[864,832]{0,1:T(8,128)} fusion(bf16[864,2560]{1,0:T(8,128)(2,1)S(1)} %copy-done, bf16[1,2560,832]{1,2,0:T(8,128)(2,1)S(1)} %bitcast.97), kind=kOutput, calls=%fused_computation.14 | convolution fusion | flops 3680501760 | bytes 11558912 | tf_op jit(solution)/shard_map/dot_general | solution.py:208
  125.3 52.9 %all-gather.3.cloned.1.call-done.rows_ref = bf16[4096,2560]{1,0:T(8,128)(2,1)} async-done(((bf16[128,2560]{1,0:T(8,128)(2,1)}), bf16[4096,2560]{1,0:T(8,128)(2,1)}) %all-gather.3.cloned.1.call-update) | async-done | bytes 20971536 | tf_op jit(solution)/shard_map/all_gather | solution.py:199
  178.3 15.0 %shard_map.119 = bf16[864,2560]{1,0:T(8,128)(2,1)} custom-call(s32[8]{0:T(128)} %fusion.45.base_ref, s32[8,1,512]{2,1,0:T(1,128)} %bitcast.87, bf16[4096,2560]{1,0:T(8,128)(2,1)} %all-gather.3.cloned.1.call-done.rows_ref), custom_call_target="tpu_custom_call" | custom-call | flops 4362076160 | bytes 25395200 | tf_op jit(solution)/shard_map/pallas_call | solution.py:80
  193.2 12.0 %multiply_reduce_fusion = (bf16[864]{0:T(1024)(128)(2,1)S(1)}, bf16[864,832]{0,1:T(8,128)(2,1)}, bf16[864,832]{0,1:T(8,128)(2,1)S(1)}, bf16[864,832]{0,1:T(8,128)(2,1)}) fusion(f32[864,832]{0,1:T(8,128)} %fusion.8, f32[864,832]{0,1:T(8,128)S(1)} %copy-done.16, f32[864]{0:T(1024)S(1)} %fusion.16, bf16[864,2560]{1,0:T(8,128)(2,1)} %shard_map.119, ...), kind=kOutput, calls=%fused_computation.20 | convolution fusion | flops 3694159104 | bytes 18752576 | tf_op jit(solution)/shard_map/dot_general | solution.py:225
  205.2 7.4 %fusion.3 = f32[864,2560]{1,0:T(8,128)} fusion(bf16[864,832]{0,1:T(8,128)(2,1)S(1)} %get-tuple-element.19, bf16[1,2560,832]{1,2,0:T(8,128)(2,1)S(1)} %bitcast.95), kind=kOutput, calls=%fused_computation.9 | convolution fusion | flops 3680501760 | bytes 14544896 | tf_op jit(solution)/shard_map/dot_general | solution.py:246
  216.1 6.3 %all-to-all-start.2 = ((bf16[32,1,128]{2,1,0:T(2,128)(2,1)}), bf16[32,1,128]{2,1,0:T(2,128)(2,1)S(1)}, u32[]{:S(2)}, u32[]{:S(2)}) async-start(bf16[32,1,128]{2,1,0:T(2,128)(2,1)} %copy.31), calls=%async_computation.2 | async-start | bytes 32768 | tf_op jit(solution)/shard_map/all_to_all | solution.py:290
  222.3 12.2 %add_convert_fusion.rows_ref = bf16[864,2560]{1,0:T(8,128)(2,1)} fusion(f32[864,2560]{1,0:T(8,128)} %fusion.3, bf16[864,832]{0,1:T(8,128)(2,1)} %get-tuple-element.20, bf16[1,2560,832]{1,2,0:T(8,128)(2,1)} %param.14), kind=kOutput, calls=%fused_computation.5 | convolution fusion | flops 3684925440 | bytes 18968576 | tf_op jit(solution)/shard_map/dot_general | solution.py:247
  234.5 10.1 %shard_map.121 = bf16[1536,2560]{1,0:T(8,128)(2,1)} custom-call(s32[32]{0:T(128)} %copy-done.11, s32[8]{0:T(128)} %fusion.46.base_ref, s32[1536,1]{1,0:T(8,128)} %add.162.row_ref, bf16[864,2560]{1,0:T(8,128)(2,1)} %add_convert_fusion.rows_ref), custom_call_target="tpu_custom_call" | custom-call | flops 1635778560 | bytes 12288000 | tf_op jit(solution)/shard_map/pallas_call | solution.py:129
  244.6 8.1 %all-to-all-start.1 = ((bf16[32,48,2560]{2,1,0:T(8,128)(2,1)}), bf16[32,48,2560]{2,1,0:T(8,128)(2,1)}, u32[]{:S(2)}, u32[]{:S(2)}) async-start(bf16[32,48,2560]{2,1,0:T(8,128)(2,1)} %bitcast.79), calls=%async_computation.1 | async-start | bytes 15728640 | tf_op jit(solution)/shard_map/all_to_all | solution.py:252
  261.9 3.8 convolution_convert_fusion.4.far_b
  268.1 5.1 %convolution_convert_fusion = bf16[832,2560]{1,0:T(8,128)(2,1)S(1)} fusion(bf16[864,832]{0,1:T(8,128)(2,1)S(1)} %copy-done.17, bf16[864,2560]{1,0:T(8,128)(2,1)S(1)} %bitcast.84, f32[864]{0:T(1024)S(1)} %fusion.16), kind=kOutput, calls=%fused_computation.7 | convolution fusion | flops 3689267200 | bytes 10124672 | tf_op jit(solution)/shard_map/dot_general | solution.py:214
  282.9 11.0 %collective-permute-done.2.low_ref = bf16[208,1280]{1,0:T(8,128)(2,1)S(1)} collective-permute-done((bf16[208,1280]{1,0:T(8,128)(2,1)S(1)}, bf16[208,1280]{1,0:T(8,128)(2,1)S(1)}, u32[]{:S(2)}, u32[]{:S(2)}) %collective-permute-start.2) | collective-permute-done | bytes 532512 | tf_op jit(solution)/shard_map/ppermute | solution.py:17
  297.6 3.3 shard_map.122
  302.3 5.3 %shard_map.123 = (bf16[1664,640]{1,0:T(8,128)(2,1)}, bf16[1664,640]{1,0:T(8,128)(2,1)}) custom-call(bf16[832,640]{1,0:T(8,128)(2,1)} %convolution_convert_fusion.7.near_a, bf16[832,640]{1,0:T(8,128)(2,1)} %convolution_convert_fusion.6.near_b, bf16[832,640]{1,0:T(8,128)(2,1)} %convolution_convert_fusion.5.far_a, ...), custom_call_target="tpu_custom_call" | custom-call | flops 1000 | bytes 1000 | tf_op jit(solution)/shard_map/pallas_call | solution.py:42
  315.1 64.3 %collective-permute-done.6 = bf16[208,2560]{1,0:T(8,128)(2,1)S(1)} collective-permute-done((bf16[208,2560]{1,0:T(8,128)(2,1)S(1)}, bf16[208,2560]{1,0:T(8,128)(2,1)S(1)}, u32[]{:S(2)}, u32[]{:S(2)}) %collective-permute-start.6) | collective-permute-done | bytes 1064992 | tf_op jit(solution)/shard_map/ppermute | solution.py:17
  382.0 4.5 %fusion.18 = bf16[1,640,832]{1,2,0:T(8,128)(2,1)} fusion(bf16[1664,640]{1,0:T(8,128)(2,1)} %collective-permute-done.5, bf16[1664,640]{1,0:T(8,128)(2,1)} %collective-permute-done.4, bf16[864,832]{0,1:T(8,128)(2,1)S(1)} %copy-done.15, bf16[864,2560]{1,0:T(8,128)(2,1)} %shard_map.120, s32[]{:T(128)S(6)} %select_n.103), kind=kOutput, calls=%fused_computation.43 | convolution fusion | flops 923852800 | bytes 5738500 | tf_op jit(solution)/shard_map/dot_general | solution.py:239
  386.5 4.3 %fusion.17 = bf16[1,640,832]{1,2,0:T(8,128)(2,1)} fusion(bf16[1664,640]{1,0:T(8,128)(2,1)} %collective-permute-done.5, bf16[1664,640]{1,0:T(8,128)(2,1)} %collective-permute-done.4, bf16[864,832]{0,1:T(8,128)(2,1)S(1)} %copy-done.13, bf16[864,2560]{1,0:T(8,128)(2,1)} %shard_map.120, s32[]{:T(128)S(6)} %select_n.103), kind=kOutput, calls=%fused_computation.42 | convolution fusion | flops 923852800 | bytes 5738500 | tf_op jit(solution)/shard_map/dot_general | solution.py:239
  390.8 5.3 %fusion.12 = bf16[128,2560]{1,0:T(8,128)(2,1)} fusion(bf16[32,48,2560]{2,1,0:T(8,128)(2,1)} %all-to-all-done.1, s32[128,32]{0,1:T(8,128)S(1)} %fusion.15), kind=kOutput, calls=%fused_computation.19 | convolution fusion | flops 1007157248 | bytes 8536064 | tf_op jit(solution)/shard_map/dot_general | solution.py:272
  (117 shorter events, 56.2 us)
Async XLA Ops:
  7.2 87.0 %all-gather.5.cloned.1.call-start = ((), (), s32[]{:S(2)}) async-start(), calls=%async_computation.4 | async-start | bytes 21626880 | tf_op jit(solution)/shard_map/all_gather | solution.py:198
  7.9 170.4 %all-gather.3.cloned.1.call-start = ((), (), s32[]{:S(2)}) async-start(), calls=%async_computation.3 | async-start | bytes 21626880 | tf_op jit(solution)/shard_map/all_gather | solution.py:199
  11.4 14.1 %all-to-all-start = ((bf16[32,1,128]{2,1,0:T(2,128)(2,1)}), bf16[32,1,128]{2,1,0:T(2,128)(2,1)S(1)}, u32[]{:S(2)}, u32[]{:S(2)}) async-start(bf16[32,1,128]{2,1,0:T(2,128)(2,1)} %copy.28), calls=%async_computation | async-start | bytes 32768 | tf_op jit(solution)/shard_map/all_to_all | solution.py:196
  42.1 52.1 %copy-start.7 = (s32[32,128]{1,0:T(8,128)}, s32[32,128]{1,0:T(8,128)S(1)}, u32[]{:S(2)}) copy-start(s32[32,128]{1,0:T(8,128)S(1)} %fusion.36) | copy-start | bytes 49156
  94.1 24.9 %slice-start.6 = ((s8[4259840]{0:T(1024)(128)(4,1)}), s8[65536]{0:T(1024)(128)(4,1)S(1)}, s32[]{:S(2)}) async-start(s8[4259840]{0:T(1024)(128)(4,1)} %bitcast.96), calls=%async_computation.11 | async-start | bytes 131072
  178.3 15.0 %copy-start.16 = (f32[864,832]{0,1:T(8,128)S(1)}, f32[864,832]{0,1:T(8,128)}, u32[]{:S(2)}) copy-start(f32[864,832]{0,1:T(8,128)} %fusion.5) | copy-start | bytes 8626180
  178.3 26.9 %slice-start.4 = ((s8[4259840]{0:T(1024)(128)(4,1)}), s8[65536]{0:T(1024)(128)(4,1)S(1)}, s32[]{:S(2)}) async-start(s8[4259840]{0:T(1024)(128)(4,1)} %bitcast.94), calls=%async_computation.9 | async-start | bytes 131072
  193.2 12.0 %slice-start.5 = ((s8[4259840]{0:T(1024)(128)(4,1)}), s8[4194304]{0:T(1024)(128)(4,1)S(1)}, s32[]{:S(2)}) async-start(s8[4259840]{0:T(1024)(128)(4,1)} %bitcast.94), calls=%async_computation.10 | async-start | bytes 8388608
  205.2 73.8 %copy-start.12 = (bf16[864,832]{0,1:T(8,128)(2,1)}, bf16[864,832]{0,1:T(8,128)(2,1)S(1)}, u32[]{:S(2)}) copy-start(bf16[864,832]{0,1:T(8,128)(2,1)S(1)} %get-tuple-element.19) | copy-start | bytes 4313092
  216.1 28.6 %all-to-all-start.2 = ((bf16[32,1,128]{2,1,0:T(2,128)(2,1)}), bf16[32,1,128]{2,1,0:T(2,128)(2,1)S(1)}, u32[]{:S(2)}, u32[]{:S(2)}) async-start(bf16[32,1,128]{2,1,0:T(2,128)(2,1)} %copy.31), calls=%async_computation.2 | async-start | bytes 32768 | tf_op jit(solution)/shard_map/all_to_all | solution.py:290
  244.6 146.2 %all-to-all-start.1 = ((bf16[32,48,2560]{2,1,0:T(8,128)(2,1)}), bf16[32,48,2560]{2,1,0:T(8,128)(2,1)}, u32[]{:S(2)}, u32[]{:S(2)}) async-start(bf16[32,48,2560]{2,1,0:T(8,128)(2,1)} %bitcast.79), calls=%async_computation.1 | async-start | bytes 15728640 | tf_op jit(solution)/shard_map/all_to_all | solution.py:252
  252.8 12.9 %slice-start = ((s8[4423680]{0:T(1024)(128)(4,1)}), s8[4194304]{0:T(1024)(128)(4,1)S(1)}, s32[]{:S(2)}) async-start(s8[4423680]{0:T(1024)(128)(4,1)} %bitcast.81), calls=%async_computation.5 | async-start | bytes 8388608
  255.6 45.3 %collective-permute-start = (bf16[832,640]{1,0:T(8,128)(2,1)S(1)}, bf16[832,640]{1,0:T(8,128)(2,1)S(1)}, u32[]{:S(2)}, u32[]{:S(2)}) collective-permute-start(bf16[832,640]{1,0:T(8,128)(2,1)S(1)} %convolution_convert_fusion.3), channel_id=1, source_target_pairs={{0,32},{32,64},{64,96},{96,0},{1,33},{33,65},{65,97},{97,1},{2,34}... | collective-permute-start | bytes 3194888 | tf_op jit(solution)/shard_map/ppermute | solution.py:17
  257.1 10.9 %slice-start.2 = ((s8[4423680]{0:T(1024)(128)(4,1)}), s8[4194304]{0:T(1024)(128)(4,1)S(1)}, s32[]{:S(2)}) async-start(s8[4423680]{0:T(1024)(128)(4,1)} %bitcast.83), calls=%async_computation.7 | async-start | bytes 8388608
  260.0 40.9 %collective-permute-start.1 = (bf16[832,640]{1,0:T(8,128)(2,1)S(1)}, bf16[832,640]{1,0:T(8,128)(2,1)S(1)}, u32[]{:S(2)}, u32[]{:S(2)}) collective-permute-start(bf16[832,640]{1,0:T(8,128)(2,1)S(1)} %convolution_convert_fusion.2), channel_id=1, source_target_pairs={{0,96},{32,0},{64,32},{96,64},{1,97},{33,1},{65,33},{97,65},{2,98}... | collective-permute-start | bytes 3194888 | tf_op jit(solution)/shard_map/ppermute | solution.py:17
  273.3 20.6 %collective-permute-start.2 = (bf16[208,1280]{1,0:T(8,128)(2,1)S(1)}, bf16[208,1280]{1,0:T(8,128)(2,1)S(1)}, u32[]{:S(2)}, u32[]{:S(2)}) collective-permute-start(bf16[208,1280]{1,0:T(8,128)(2,1)S(1)} %get-tuple-element.22), channel_id=1, source_target_pairs={{0,32},{32,64},{64,96},{96,0},{1,33},{33,65},{65,97},{97,1},{2,34}... | collective-permute-start | bytes 1597448 | tf_op jit(solution)/shard_map/ppermute | solution.py:17
  273.5 23.2 %collective-permute-start.3 = (bf16[208,1280]{1,0:T(8,128)(2,1)S(1)}, bf16[208,1280]{1,0:T(8,128)(2,1)S(1)}, u32[]{:S(2)}, u32[]{:S(2)}) collective-permute-start(bf16[208,1280]{1,0:T(8,128)(2,1)S(1)} %get-tuple-element.21), channel_id=1, source_target_pairs={{0,96},{32,0},{64,32},{96,64},{1,97},{33,1},{65,33},{97,65},{2,98}... | collective-permute-start | bytes 1597448 | tf_op jit(solution)/shard_map/ppermute | solution.py:17
  302.3 11.9 %copy-start.10 = (s32[128,6]{0,1:T(8,128)S(1)}, s32[128,6]{0,1:T(8,128)}, u32[]{:S(2)}) copy-start(s32[128,6]{0,1:T(8,128)} %param.10) | copy-start | bytes 9220
  302.3 12.2 %copy-start.9 = (f32[128,6]{0,1:T(8,128)S(1)}, f32[128,6]{0,1:T(8,128)}, u32[]{:S(2)}) copy-start(f32[128,6]{0,1:T(8,128)} %param.11) | copy-start | bytes 9220
  307.6 74.4 %collective-permute-start.4 = (bf16[1664,640]{1,0:T(8,128)(2,1)}, bf16[1664,640]{1,0:T(8,128)(2,1)}, u32[]{:S(2)}, u32[]{:S(2)}) collective-permute-start(bf16[1664,640]{1,0:T(8,128)(2,1)} %get-tuple-element.10), channel_id=1, source_target_pairs={{0,32},{32,64},{64,96},{96,0},{1,33},{33,65},{65,97},{97,1},{2,34}... | collective-permute-start | bytes 6389768 | tf_op jit(solution)/shard_map/ppermute | solution.py:17
  309.2 72.8 %collective-permute-start.5 = (bf16[1664,640]{1,0:T(8,128)(2,1)}, bf16[1664,640]{1,0:T(8,128)(2,1)}, u32[]{:S(2)}, u32[]{:S(2)}) collective-permute-start(bf16[1664,640]{1,0:T(8,128)(2,1)} %get-tuple-element.11), channel_id=1, source_target_pairs={{0,96},{32,0},{64,32},{96,64},{1,97},{33,1},{65,33},{97,65},{2,98}... | collective-permute-start | bytes 6389768 | tf_op jit(solution)/shard_map/ppermute | solution.py:17
  311.0 68.4 %collective-permute-start.6 = (bf16[208,2560]{1,0:T(8,128)(2,1)S(1)}, bf16[208,2560]{1,0:T(8,128)(2,1)S(1)}, u32[]{:S(2)}, u32[]{:S(2)}) collective-permute-start(bf16[208,2560]{1,0:T(8,128)(2,1)S(1)} %copy-done.2), channel_id=1, source_target_pairs={{0,32},{32,64},{64,96},{96,0},{1,33},{33,65},{65,97},{97,1},{2,34}... | collective-permute-start | bytes 3194888 | tf_op jit(solution)/shard_map/ppermute | solution.py:17
  311.3 68.1 %collective-permute-start.7 = (bf16[208,2560]{1,0:T(8,128)(2,1)}, bf16[208,2560]{1,0:T(8,128)(2,1)S(1)}, u32[]{:S(2)}, u32[]{:S(2)}) collective-permute-start(bf16[208,2560]{1,0:T(8,128)(2,1)} %get-tuple-element.12), channel_id=1, source_target_pairs={{0,96},{32,0},{64,32},{96,64},{1,97},{33,1},{65,33},{97,65},{2,98}... | collective-permute-start | bytes 3194888 | tf_op jit(solution)/shard_map/ppermute | solution.py:17
  315.1 66.9 %copy-start.15 = (bf16[864,832]{0,1:T(8,128)(2,1)S(1)}, bf16[864,832]{0,1:T(8,128)(2,1)}, u32[]{:S(2)}) copy-start(bf16[864,832]{0,1:T(8,128)(2,1)} %get-tuple-element.20) | copy-start | bytes 4313092
  (15 other events, 84.2 us)
Sparse Core Ops, SparseCore 0:
  10.2 83.8 all-gather.4
  96.4 81.8 all-gather.2
where the time goes:
time: 408 us; the launch traced here: 403 us
  waiting for transfers between devices  185 us (45%)
  matrix products  86.5 us (21%)
  Pallas kernels  48.7 us (12%)
  starting transfers between devices  35.7 us (9%)
  between operations  15.9 us (4%)
  other arithmetic  12.3 us (3%)
  local copies, waits for them, and re-layouts  10.5 us (3%)
  blocking collectives  9.08 us (2%)
    ppermute x8, waiting for transfers between devices, along_y(): return lax.ppermute(v, 'dp', [(r, (r + by) % N_REP) for r in range(N_REP)])  78.2 us
    all_gather x1, waiting for transfers between devices, local(): dy_all = lax.all_gather(cotangent, 'expert', axis=0, tiled=True)  52.9 us
    all_gather x1, waiting for transfers between devices, local(): x_all = lax.all_gather(tokens, 'expert', axis=0, tiled=True)  48.5 us
    pallas_call x2, Pallas kernels, pick(): pl.pallas_call(functools.partial(pick_kernel, most, min(512, width)), gri...  29.9 us
    dot_general x8, matrix products, weight_term(): lax.dot_general(grad, columns[d], (((0,), (0,)), ((), ())), preferred_ele...  25.6 us
    ppermute x8, starting transfers between devices, along_y(): return lax.ppermute(v, 'dp', [(r, (r + by) % N_REP) for r in range(N_REP)])  13.3 us
    dot_general x1, matrix products, local(): lax.dot_general(grad_lifted, upper, (((1,), (1,)), ((), ())), preferred_e...  12.2 us
    dot_general x1, matrix products, local(): lax.dot_general(cot_rows, lower, (((1,), (1,)), ((), ())), preferred_elem...  12 us
  transfers between devices with their start and end apart: 13, of which 6 were waited for; matrix products, arithmetic and copies ran while one was open for 20% of the time, Pallas kernels for 8%

commit v1 on v0

v1 whole, which is shorter than its diff:
```python
import functools

import jax
import jax.numpy as jnp
from jax import lax
from jax.experimental import pallas as pl
from jax.experimental.pallas import tpu as pltpu
from jax.sharding import PartitionSpec as P

BF = jnp.bfloat16
F32 = jnp.float32
N_REP = 4
N_EXP = 32


LANES = 128
VMEM_LIMIT = 56 * 1024 * 1024


def pick_kernel(most, tile, base_ref, slot_ref, rows_ref, out_ref, acc):
    group = pl.program_id(0)
    slots, width = out_ref.shape

    @pl.when(group == 0)
    def _():
        acc[...] = jnp.zeros_like(acc)

    base = pl.multiple_of(base_ref[group], 16)
    iota = lax.broadcasted_iota(jnp.int32, (most, rows_ref.shape[0]), 0) + base
    hot = (iota == slot_ref[...]).astype(BF)
    at = pl.ds(base, most)
    for w in range(0, width, tile):
        part = jnp.dot(hot, rows_ref[:, w : w + tile], preferred_element_type=F32)
        acc[at, w : w + tile] = acc[at, w : w + tile] + part.astype(BF)

    @pl.when(group == pl.num_programs(0) - 1)
    def _():
        out_ref[...] = acc[:slots, :]


def pick(rows, slot, first, slots, most_block, blocks):
    tokens, width = rows.shape
    count = tokens // first.shape[0]
    groups = first.shape[0] // blocks
    most = blocks * most_block + 16
    base = jnp.minimum(first.reshape(groups, blocks)[:, 0], slots) // 16 * 16
    return pl.pallas_call(
        functools.partial(pick_kernel, most, min(512, width)),
        grid_spec=pltpu.PrefetchScalarGridSpec(
            num_scalar_prefetch=1,
            grid=(groups,),
            in_specs=[
                pl.BlockSpec((None, 1, blocks * count), lambda g, base: (g, 0, 0)),
                pl.BlockSpec((blocks * count, width), lambda g, base: (g, 0)),
            ],
            out_specs=pl.BlockSpec((slots, width), lambda g, base: (0, 0)),
            scratch_shapes=[pltpu.VMEM((slots + most, width), BF)],
        ),
        out_shape=jax.ShapeDtypeStruct((slots, width), BF),
        compiler_params=pltpu.CompilerParams(vmem_limit_bytes=VMEM_LIMIT),
        cost_estimate=pl.CostEstimate(
            flops=2 * most * tokens * width,
            bytes_accessed=2 * width * (tokens + slots),
            transcendentals=0,
        ),
    )(base, slot.reshape(groups, 1, blocks * count), rows)


def back_kernel(
    most_block, width, first_ref, hidden_ref, lifted_ref, gate_ref, upper_ref, share_ref, *refs
):
    out_ref, rows = refs[-2], refs[-1]
    slots = hidden_ref.shape[0]

    @pl.when(pl.program_id(0) == 0)
    def _():
        rows[slots:, :] = jnp.zeros((rows.shape[0] - slots, rows.shape[1]), F32)

    step = slots // 2

    @pl.loop(0, 2)
    def _(m):
        at = pl.ds(pl.multiple_of(m * step, 16), step)
        total = jnp.dot(hidden_ref[at, :], gate_ref[...], preferred_element_type=F32)
        rows[at, :] = total + jnp.dot(
            lifted_ref[at, :], upper_ref[...], preferred_element_type=F32
        )

    at_share = width % out_ref.shape[2]

    @pl.when(pl.program_id(0) == pl.num_programs(0) - 1)
    def _():
        rows[:slots, at_share:] = jnp.broadcast_to(
            share_ref[...], (slots, out_ref.shape[2] - at_share)
        )

    @pl.loop(0, out_ref.shape[0], unroll=4)
    def _(block):
        first = first_ref[block]
        base = pl.multiple_of(first // 8 * 8, 8)
        window = rows[pl.ds(base, most_block + 8), :]
        window = pltpu.roll(window, (most_block + 8 - (first - base)) % (most_block + 8), 0)
        out_ref[block] = window[:most_block].astype(BF)


def back_blocks(grad_hidden, grad_lifted, gate, upper, shares, first, most_block, deps):
    slots, ff = grad_hidden.shape
    width = gate.shape[1]
    steps = 3
    tile = (width + LANES) // steps
    blocks = first.shape[0]
    assert tile % LANES == 0 and tile * (steps - 1) < width
    return pl.pallas_call(
        functools.partial(back_kernel, most_block, width),
        grid_spec=pltpu.PrefetchScalarGridSpec(
            num_scalar_prefetch=1,
            grid=(steps,),
            in_specs=[pl.BlockSpec((slots, ff), lambda j, _: (0, 0))] * 2
            + [pl.BlockSpec((ff, tile), lambda j, _: (0, j))] * 2
            + [pl.BlockSpec((slots, 1), lambda j, _: (0, 0))]
            + [pl.BlockSpec(memory_space=pl.ANY)] * len(deps),
            out_specs=pl.BlockSpec((blocks, most_block, tile), lambda j, _: (0, 0, j)),
            scratch_shapes=[pltpu.VMEM((slots + most_block + 16, tile), F32)],
        ),
        out_shape=jax.ShapeDtypeStruct((blocks, most_block, width + LANES), BF),
        compiler_params=pltpu.CompilerParams(vmem_limit_bytes=VMEM_LIMIT),
        cost_estimate=pl.CostEstimate(
            flops=4 * slots * ff * width,
            bytes_accessed=4 * width * (ff + blocks * most_block),
            transcendentals=0,
        ),
    )(jnp.minimum(first, slots), grad_hidden, grad_lifted, gate, upper, shares[:, None], *deps)


def grads_kernel(hidden_ref, lifted_ref, rows_ref, *refs):
    out_a, out_b, left = refs[-3:]

    @pl.when(pl.program_id(0) == 0)
    def _():
        left[0] = hidden_ref[...].T
        left[1] = lifted_ref[...].T

    for n, out in enumerate((out_a, out_b)):
        out[...] = jnp.dot(left[n], rows_ref[...], preferred_element_type=F32).astype(BF)


def grads(grad_hidden, grad_lifted, rows, deps):
    slots, ff = grad_hidden.shape
    cut = rows.shape[1] // N_REP
    fixed = pl.BlockSpec((slots, ff), lambda d: (0, 0))
    return pl.pallas_call(
        grads_kernel,
        grid=(N_REP,),
        in_specs=[
            fixed,
            fixed,
            pl.BlockSpec((slots, cut), lambda d: (0, d)),
        ]
        + [pl.BlockSpec(memory_space=pl.ANY)] * len(deps),
        out_specs=[pl.BlockSpec((ff, cut), lambda d: (d, 0))] * 2,
        out_shape=[jax.ShapeDtypeStruct((N_REP * ff, cut), BF)] * 2,
        scratch_shapes=[pltpu.VMEM((2, ff, slots), BF)],
        compiler_params=pltpu.CompilerParams(vmem_limit_bytes=VMEM_LIMIT),
        cost_estimate=pl.CostEstimate(
            flops=4 * slots * ff * rows.shape[1],
            bytes_accessed=2 * rows.shape[1] * (slots + 2 * ff),
            transcendentals=0,
        ),
    )(grad_hidden, grad_lifted, rows, *deps)


def one_hot(slot, slots):
    return (lax.broadcasted_iota(jnp.int32, (slots, slot.shape[0]), 0) == slot[None, :]).astype(BF)


def placement(weight, spares, rep, cap, spare_cap):
    named = weight > 0
    load = jnp.sum(named.astype(jnp.int32))
    load = lax.all_gather(jnp.broadcast_to(load, (1, 128)), "dp", axis=0, tiled=True)[:, 0]
    excess = jnp.maximum(load - cap, 0)
    iota = jnp.arange(N_REP, dtype=jnp.int32)
    same = spares == spares[rep]
    offset = jnp.sum(jnp.where(same & (iota < rep) & (spares != iota), excess, 0))
    extra = jnp.where(spares[rep] != rep, jnp.maximum(spare_cap - offset, 0), 0)
    running, totals = running_count(named)
    before = jnp.cumsum(totals) - totals
    position = before[:, None] + running - 1
    placed = named & (position < cap + extra)
    return jnp.where(placed, position, -1), before


def running_count(named):
    count = named.shape[-1]
    upto = (
        lax.broadcasted_iota(jnp.int32, (count, count), 0)
        <= lax.broadcasted_iota(jnp.int32, (count, count), 1)
    ).astype(BF)
    running = jnp.dot(named.astype(BF), upto, preferred_element_type=F32).astype(jnp.int32)
    return running, running[:, -1]


def local(tokens, cotangent, expert_ids, router_probs, spare_replica, w_gate, w_up, w_down):
    rep = lax.axis_index("dp")
    count, width = tokens.shape
    top = expert_ids.shape[1]
    cap = count * top
    spare_cap = cap // 8
    slots = cap + spare_cap
    gate, upper, lower = w_gate[0], w_up[0], w_down[0]
    ff = gate.shape[1]
    total = jnp.sum(router_probs, axis=1, keepdims=True)
    scale = router_probs / total
    scale_b = scale.astype(BF)

    named_here = expert_ids.T[None] == jnp.arange(N_EXP, dtype=jnp.int32)[:, None, None]
    weight = jnp.sum(jnp.where(named_here, scale_b.T.astype(F32)[None], 0.0), axis=1).astype(BF)
    weight = lax.all_to_all(weight, "expert", split_axis=0, concat_axis=0, tiled=True)

    x_all = lax.all_gather(tokens, "expert", axis=0, tiled=True)
    dy_all = lax.all_gather(cotangent, "expert", axis=0, tiled=True)

    slot, first = placement(weight, spare_replica[0], rep, cap, spare_cap)

    chosen = one_hot(slot.reshape(-1), slots)
    row_scale = jnp.dot(chosen, weight.reshape(-1, 1), preferred_element_type=F32)
    most_block = min(count, 2 * count * top // N_EXP)
    rows_in = pick(x_all, slot.reshape(-1), first, slots, most_block, 4)
    hidden = jnp.dot(rows_in, gate, preferred_element_type=F32)
    lifted = jnp.dot(rows_in, upper, preferred_element_type=F32)
    logistic = jax.nn.sigmoid(hidden)
    swished = hidden * logistic
    activated = (swished * lifted).astype(BF)
    cot_rows = pick(dy_all, slot.reshape(-1), first, slots, most_block, 4)
    grad_out = (row_scale * cot_rows.astype(F32)).astype(BF)
    part_lower = lax.dot_general(
        activated, grad_out, (((0,), (0,)), ((), ())), preferred_element_type=F32
    ).astype(BF)
    grad_lower = lax.psum_scatter(part_lower, "dp", scatter_dimension=0, tiled=True)

    pulled = lax.dot_general(
        cot_rows, lower, (((1,), (1,)), ((), ())), preferred_element_type=F32
    )
    shares = jnp.sum(activated.astype(F32) * pulled, axis=1)
    grad_act = row_scale * pulled
    grad_hidden = (grad_act * lifted * logistic * (1.0 + hidden * (1.0 - logistic))).astype(BF)
    grad_lifted = (grad_act * swished).astype(BF)

    gate_parts, upper_parts = grads(grad_hidden, grad_lifted, rows_in, (part_lower,))
    grad_gate = lax.psum_scatter(gate_parts, "dp", scatter_dimension=0, tiled=True)
    grad_upper = lax.psum_scatter(upper_parts, "dp", scatter_dimension=0, tiled=True)

    packed = back_blocks(
        grad_hidden,
        grad_lifted,
        gate.T,
        upper.T,
        shares,
        first,
        most_block,
        (gate_parts, upper_parts),
    )
    came = lax.all_to_all(packed, "expert", split_axis=0, concat_axis=0, tiled=True)

    named_any = jnp.any(named_here, axis=1)
    rank = jnp.where(named_any, running_count(named_any)[0] - 1, -1).T
    hot = rank[:, :, None] == jnp.arange(most_block, dtype=jnp.int32)[None, None, :]
    token_grad = jnp.dot(
        hot.reshape(count, -1).astype(BF),
        came.reshape(-1, width + LANES),
        preferred_element_type=F32,
    )[:, :width].astype(BF)
    share_all = jnp.sum(jnp.where(hot, came[:, :, width].astype(F32)[None], 0.0), axis=2)
    mine = expert_ids[:, :, None] == jnp.arange(N_EXP, dtype=jnp.int32)[None, None, :]
    share = jnp.sum(jnp.where(mine, share_all[:, None, :], 0.0), axis=2)
    prob_grad = (share - jnp.sum(scale * share, axis=1, keepdims=True)) / total

    return (
        token_grad,
        prob_grad,
        grad_gate.T[None],
        grad_upper.T[None],
        grad_lower[None],
    )


def solution(mesh):
    return jax.shard_map(
        local,
        mesh=mesh,
        in_specs=(
            P(("dp", "expert"), None),
            P(("dp", "expert"), None),
            P(("dp", "expert"), None),
            P(("dp", "expert"), None),
            P("expert", None),
            P("expert", None, None),
            P("expert", None, None),
            P("expert", None, None),
        ),
        out_specs=(
            P(("dp", "expert"), None),
            P(("dp", "expert"), None),
            P("expert", "dp", None),
            P("expert", "dp", None),
            P("expert", "dp", None),
        ),
        check_vma=False,
    )
```

time: 408 us -> 393 us (0.963)
  matrix products: 86.5 us -> 38.2 us
  waiting for transfers between devices: 185 us -> 233 us
  starting transfers between devices: 35.7 us -> 14.6 us
  Pallas kernels: 48.7 us -> 67 us
    all_to_all x1, waiting for transfers between devices: 0.01 us -> 121 us  [local(): lax.all_to_all(packed, 'expert', split_axis=0, concat_axis=0, tiled=True)]
    ppermute x8 -> x0, waiting for transfers between devices: 78.2 us -> none  [along_y(): return lax.ppermute(v, 'dp', [(r, (r + by) % N_REP) for r in range(N_REP)])]
    dot_general x11 -> x1, matrix products: 50.5 us -> 4.71 us  [local(): jnp.dot(hot.reshape(count, -1).astype(BF), came.reshape(-1, width + LANES...]
    pallas_call x3 -> x2, Pallas kernels: 18.7 us -> 36.8 us  [the longest x1 21.8 us: back_blocks(): pl.pallas_call(functools.partial(back_kernel, most_block, width), grid_sp...]
    ppermute x8 -> x0, starting transfers between devices: 13.3 us -> none  [along_y(): return lax.ppermute(v, 'dp', [(r, (r + by) % N_REP) for r in range(N_REP)])]
    all_to_all x1 -> x0, starting transfers between devices: 6.26 us -> none  [local(): lax.all_to_all(share_rows.reshape(N_EXP, count), 'expert', split_axis=0,...]
  transfers between devices with their start and end apart: 13 -> 7, of which waited for: 6 -> 4; matrix products, arithmetic and copies ran while one was open for 20% -> 9% of each run, Pallas kernels for 8% -> 9%
where the time goes in v1:
time: 393 us; the launch traced here: 392 us
  waiting for transfers between devices  233 us (59%)
  Pallas kernels  67 us (17%)
  matrix products  38.2 us (10%)
  between operations  15.3 us (4%)
  starting transfers between devices  14.6 us (4%)
  blocking collectives  9.08 us (2%)
  other arithmetic  8.39 us (2%)
  local copies, waits for them, and re-layouts  6.61 us (2%)
    all_to_all x1, waiting for transfers between devices, local(): lax.all_to_all(packed, 'expert', split_axis=0, concat_axis=0, tiled=True)  121 us
    all_gather x1, waiting for transfers between devices, local(): dy_all = lax.all_gather(cotangent, 'expert', axis=0, tiled=True)  55.3 us
    all_gather x1, waiting for transfers between devices, local(): x_all = lax.all_gather(tokens, 'expert', axis=0, tiled=True)  50 us
    pallas_call x2, Pallas kernels, pick(): pl.pallas_call(functools.partial(pick_kernel, most, min(512, width)), gri...  30.3 us
    pallas_call x1, Pallas kernels, back_blocks(): pl.pallas_call(functools.partial(back_kernel, most_block, width), grid_sp...  21.8 us
    pallas_call x1, Pallas kernels, grads(): pl.pallas_call(grads_kernel, grid=(N_REP,), in_specs=[fixed, fixed, pl.Bl...  15 us
    dot_general x1, matrix products, local(): lax.dot_general(cot_rows, lower, (((1,), (1,)), ((), ())), preferred_elem...  11 us
    unnamed x1, blocking collectives  9.08 us
  transfers between devices with their start and end apart: 7, of which 4 were waited for; matrix products, arithmetic and copies ran while one was open for 9% of the time, Pallas kernels for 9%

profile of v1, /device:TPU:32, one launch (start us, length us, event | category | flops | bytes accessed | tf_op | source)
XLA Modules:
  0.0 391.8 jit_solution(3059936407296717520)
XLA Ops:
  11.4 8.0 %all-to-all-start = ((bf16[32,1,128]{2,1,0:T(2,128)(2,1)}), bf16[32,1,128]{2,1,0:T(2,128)(2,1)S(1)}, u32[]{:S(2)}, u32[]{:S(2)}) async-start(bf16[32,1,128]{2,1,0:T(2,128)(2,1)} %copy.63), calls=%async_computation | async-start | bytes 32768 | tf_op jit(solution)/shard_map/all_to_all | solution.py:217
  19.5 1.2 constant_dynamic-slice_fusion
  20.7 1.2 dynamic-slice.1
  22.0 3.5 all-to-all-done
  26.1 1.4 dynamic-update-slice
  28.2 9.1 %all-reduce = s32[4]{0:T(128)S(1)} all-reduce(s32[4]{0:T(128)S(1)} %dynamic-update-slice), channel_id=2, replica_groups=mesh['dp'=4,'expert'=32] {'dp'}, use_global_device_ids=true, to_apply=%add | all-reduce | flops 4 | bytes 32
  38.3 1.9 fusion.19
  41.1 2.5 fusion.12
  44.1 50.0 %all-gather.5.cloned.1.call-done.rows_ref = bf16[4096,2560]{1,0:T(8,128)(2,1)} async-done(((bf16[128,2560]{1,0:T(8,128)(2,1)}), bf16[4096,2560]{1,0:T(8,128)(2,1)}) %all-gather.5.cloned.1.call-update) | async-done | bytes 20971536 | tf_op jit(solution)/shard_map/all_gather | solution.py:219
  94.1 15.4 %shard_map.120.rows_ref = bf16[864,2560]{1,0:T(8,128)(2,1)} custom-call(s32[8]{0:T(128)} %fusion.18.base_ref, s32[8,1,512]{2,1,0:T(1,128)} %bitcast.64, bf16[4096,2560]{1,0:T(8,128)(2,1)} %all-gather.5.cloned.1.call-done.rows_ref), custom_call_target="tpu_custom_call" | custom-call | flops 4362076160 | bytes 25395200 | tf_op jit(solution)/shard_map/pallas_call | solution.py:47
  109.5 6.9 %fusion.5 = f32[864,832]{1,0:T(8,128)S(1)} fusion(bf16[864,2560]{1,0:T(8,128)(2,1)} %shard_map.120.rows_ref, bf16[1,2560,832]{1,2,0:T(8,128)(2,1)S(1)} %bitcast.59), kind=kOutput, calls=%fused_computation.8 | convolution fusion | flops 3680501760 | bytes 11558912 | tf_op jit(solution)/shard_map/dot_general | solution.py:229
  116.5 6.5 %fusion.3 = f32[864,832]{1,0:T(8,128)} fusion(bf16[864,2560]{1,0:T(8,128)(2,1)S(1)} %copy-done, bf16[1,2560,832]{1,2,0:T(8,128)(2,1)S(1)} %bitcast.62), kind=kOutput, calls=%fused_computation.6 | convolution fusion | flops 3680501760 | bytes 11558912 | tf_op jit(solution)/shard_map/dot_general | solution.py:228
  122.9 55.3 %all-gather.3.cloned.1.call-done.rows_ref = bf16[4096,2560]{1,0:T(8,128)(2,1)} async-done(((bf16[128,2560]{1,0:T(8,128)(2,1)}), bf16[4096,2560]{1,0:T(8,128)(2,1)}) %all-gather.3.cloned.1.call-update) | async-done | bytes 20971536 | tf_op jit(solution)/shard_map/all_gather | solution.py:220
  178.2 14.9 %shard_map.119 = bf16[864,2560]{1,0:T(8,128)(2,1)} custom-call(s32[8]{0:T(128)} %fusion.18.base_ref, s32[8,1,512]{2,1,0:T(1,128)} %bitcast.65, bf16[4096,2560]{1,0:T(8,128)(2,1)} %all-gather.3.cloned.1.call-done.rows_ref), custom_call_target="tpu_custom_call" | custom-call | flops 4362076160 | bytes 25395200 | tf_op jit(solution)/shard_map/pallas_call | solution.py:47
  193.1 11.0 %multiply_reduce_fusion = (f32[864]{0:T(1024)S(1)}, bf16[864,832]{1,0:T(8,128)(2,1)S(1)}, bf16[864,832]{1,0:T(8,128)(2,1)}, bf16[864,832]{1,0:T(8,128)(2,1)}) fusion(f32[864,832]{1,0:T(8,128)S(1)} %fusion.5, f32[864,832]{1,0:T(8,128)S(1)} %copy-done.5, f32[864]{0:T(1024)S(1)} %fusion.12, bf16[864,2560]{1,0:T(8,128)(2,1)} %shard_map.119, ...), kind=kOutput, calls=%fused_computation.13 | convolution fusion | flops 3694159104 | bytes 18754304 | tf_op jit(solution)/shard_map/dot_general | solution.py:240
  204.1 6.4 %convolution_convert_fusion.refs_0_ = bf16[832,2560]{1,0:T(8,128)(2,1)} fusion(bf16[864,832]{1,0:T(8,128)(2,1)S(1)} %get-tuple-element.12, bf16[864,2560]{1,0:T(8,128)(2,1)S(1)} %copy-done.1, f32[864]{0:T(1024)S(1)} %fusion.12), kind=kOutput, calls=%fused_computation.4 | convolution fusion | flops 3689267200 | bytes 10124672 | tf_op jit(solution)/shard_map/dot_general | solution.py:235
  210.5 15.0 %shard_map.121 = (bf16[3328,640]{1,0:T(8,128)(2,1)}, bf16[3328,640]{1,0:T(8,128)(2,1)}) custom-call(bf16[864,832]{1,0:T(8,128)(2,1)} %get-tuple-element.15.hidden_ref, bf16[864,832]{1,0:T(8,128)(2,1)} %get-tuple-element.16.lifted_ref, bf16[864,2560]{1,0:T(8,128)(2,1)} %shard_map.120.rows_ref, bf16[832,2560]{1,0:T(8,128)(2,1)} %convolution_convert_fusion.refs_0_), custom_call_target="tpu_custom_call" | custom-call | flops 7361003520 | bytes 12943360 | tf_op jit(solution)/shard_map/pallas_call | solution.py:151
  226.1 0.9 broadcast_in_dim.79.share_ref
  227.0 21.8 %shard_map.122 = bf16[32,48,2688]{2,1,0:T(8,128)(2,1)} custom-call(s32[32]{0:T(128)} %get-tuple-element.10.first_ref, bf16[864,832]{1,0:T(8,128)(2,1)} %get-tuple-element.15.hidden_ref, bf16[864,832]{1,0:T(8,128)(2,1)} %get-tuple-element.16.lifted_ref, bf16[832,2560]{1,0:T(8,128)(2,1)} %bitcast.60, bf16[832,2560]{1,0:T(8,128)(2,1)} %bitcast.57, ...), custom_call_target="tpu_custom_call" | custom-call | flops 7361003520 | bytes 24248320 | tf_op jit(solution)/shard_map/pallas_call | solution.py:113
  248.8 6.3 %all-to-all-start.1 = ((bf16[32,48,2688]{2,1,0:T(8,128)(2,1)}), bf16[32,48,2688]{2,1,0:T(8,128)(2,1)}, u32[]{:S(2)}, u32[]{:S(2)}) async-start(bf16[32,48,2688]{2,1,0:T(8,128)(2,1)} %shard_map.122), calls=%async_computation.1 | async-start | bytes 16515072 | tf_op jit(solution)/shard_map/all_to_all | solution.py:262
  256.0 121.4 %all-to-all-done.1 = bf16[32,48,2688]{2,1,0:T(8,128)(2,1)} async-done(((bf16[32,48,2688]{2,1,0:T(8,128)(2,1)}), bf16[32,48,2688]{2,1,0:T(8,128)(2,1)}, u32[]{:S(2)}, u32[]{:S(2)}) %all-to-all-start.1) | async-done | bytes 8257568 | tf_op jit(solution)/shard_map/all_to_all | solution.py:262
  377.4 4.7 %convolution_bitcast_fusion = bf16[128,2688]{1,0:T(8,128)(2,1)S(1)} fusion(bf16[32,48,2688]{2,1,0:T(8,128)(2,1)} %all-to-all-done.1, s32[128,32]{0,1:T(8,128)S(1)} %fusion.11), kind=kOutput, calls=%fused_computation.12 | convolution fusion | flops 1057161216 | bytes 8962048 | tf_op jit(solution)/shard_map/dot_general | solution.py:267
  382.1 0.9 slice.30
  383.0 1.3 convert_reduce_fusion
  (55 shorter events, 9.0 us)
Async XLA Ops:
  7.2 86.9 %all-gather.5.cloned.1.call-start = ((), (), s32[]{:S(2)}) async-start(), calls=%async_computation.6 | async-start | bytes 21626880 | tf_op jit(solution)/shard_map/all_gather | solution.py:219
  7.9 170.3 %all-gather.3.cloned.1.call-start = ((), (), s32[]{:S(2)}) async-start(), calls=%async_computation.5 | async-start | bytes 21626880 | tf_op jit(solution)/shard_map/all_gather | solution.py:220
  11.4 14.1 %all-to-all-start = ((bf16[32,1,128]{2,1,0:T(2,128)(2,1)}), bf16[32,1,128]{2,1,0:T(2,128)(2,1)S(1)}, u32[]{:S(2)}, u32[]{:S(2)}) async-start(bf16[32,1,128]{2,1,0:T(2,128)(2,1)} %copy.63), calls=%async_computation | async-start | bytes 32768 | tf_op jit(solution)/shard_map/all_to_all | solution.py:217
  19.4 365.8 %reduce-scatter.4.cloned.1.call-start = ((), (), s32[]{:S(2)}) async-start(), calls=%async_computation.7 | async-start | bytes 5324800 | tf_op jit(solution)/shard_map/reduce_scatter | solution.py:249
  41.1 53.0 %copy-start.2 = (s32[32,128]{1,0:T(8,128)}, s32[32,128]{1,0:T(8,128)S(1)}, u32[]{:S(2)}) copy-start(s32[32,128]{1,0:T(8,128)S(1)} %fusion.17) | copy-start | bytes 49156
  41.1 68.4 %slice-start = ((s8[4259840]{0:T(1024)(128)(4,1)}), s8[65536]{0:T(1024)(128)(4,1)S(1)}, s32[]{:S(2)}) async-start(s8[4259840]{0:T(1024)(128)(4,1)} %bitcast.58), calls=%async_computation.10 | async-start | bytes 131072
  94.1 15.4 %slice-start.1 = ((s8[4259840]{0:T(1024)(128)(4,1)}), s8[4194304]{0:T(1024)(128)(4,1)S(1)}, s32[]{:S(2)}) async-start(s8[4259840]{0:T(1024)(128)(4,1)} %bitcast.58), calls=%async_computation.11 | async-start | bytes 8388608
  94.1 22.3 %slice-start.2 = ((s8[4259840]{0:T(1024)(128)(4,1)}), s8[65536]{0:T(1024)(128)(4,1)S(1)}, s32[]{:S(2)}) async-start(s8[4259840]{0:T(1024)(128)(4,1)} %bitcast.61), calls=%async_computation.12 | async-start | bytes 131072
  109.5 7.0 %copy-start = (bf16[864,2560]{1,0:T(8,128)(2,1)S(1)}, bf16[864,2560]{1,0:T(8,128)(2,1)}, u32[]{:S(2)}) copy-start(bf16[864,2560]{1,0:T(8,128)(2,1)} %shard_map.120.rows_ref) | copy-start | bytes 13271044
  109.5 7.0 %slice-start.3 = ((s8[4259840]{0:T(1024)(128)(4,1)}), s8[4194304]{0:T(1024)(128)(4,1)S(1)}, s32[]{:S(2)}) async-start(s8[4259840]{0:T(1024)(128)(4,1)} %bitcast.61), calls=%async_computation.13 | async-start | bytes 8388608
  178.2 14.9 %copy-start.5 = (f32[864,832]{1,0:T(8,128)S(1)}, f32[864,832]{1,0:T(8,128)}, u32[]{:S(2)}) copy-start(f32[864,832]{1,0:T(8,128)} %fusion.3) | copy-start | bytes 8626180
  193.1 11.0 %copy-start.1 = (bf16[864,2560]{1,0:T(8,128)(2,1)S(1)}, bf16[864,2560]{1,0:T(8,128)(2,1)}, u32[]{:S(2)}) copy-start(bf16[864,2560]{1,0:T(8,128)(2,1)} %shard_map.119) | copy-start | bytes 13271044
  225.5 159.7 %reduce-scatter.6.cloned.1.call-start = ((), (), s32[]{:S(2)}) async-start(), calls=%async_computation.8 | async-start | bytes 5324800 | tf_op jit(solution)/shard_map/reduce_scatter | solution.py:250
  248.8 128.6 %all-to-all-start.1 = ((bf16[32,48,2688]{2,1,0:T(8,128)(2,1)}), bf16[32,48,2688]{2,1,0:T(8,128)(2,1)}, u32[]{:S(2)}, u32[]{:S(2)}) async-start(bf16[32,48,2688]{2,1,0:T(8,128)(2,1)} %shard_map.122), calls=%async_computation.1 | async-start | bytes 16515072 | tf_op jit(solution)/shard_map/all_to_all | solution.py:262
  255.2 0.7 copy-start.4
  255.2 130.1 %reduce-scatter.8.cloned.1.call-start = ((), (), s32[]{:S(2)}) async-start(), calls=%async_computation.9 | async-start | bytes 5324800 | tf_op jit(solution)/shard_map/reduce_scatter | solution.py:238
  256.0 128.6 %copy-start.3 = (f32[128,6]{0,1:T(8,128)S(1)}, f32[128,6]{0,1:T(8,128)}, u32[]{:S(2)}) copy-start(f32[128,6]{0,1:T(8,128)} %param.11) | copy-start | bytes 9220
Sparse Core Ops, SparseCore 0:
  10.2 83.8 all-gather.4
  96.4 81.8 all-gather.2
  225.6 47.4 reduce-scatter.3
  276.1 47.0 reduce-scatter.5
  326.0 47.0 reduce-scatter.7

commit v2 on v1

--- a/solution.py
+++ b/solution.py
@@ -14,7 +14,32 @@
 
 
 LANES = 128
+
+
+def along_y(v, by):
+    return lax.ppermute(v, "dp", [(r, (r + by) % N_REP) for r in range(N_REP)])
+
+
 VMEM_LIMIT = 56 * 1024 * 1024
+
+
+def join_wide_kernel(near_ref, far_ref, low_ref, high_ref, dep_ref, ahead_ref, behind_ref):
+    half = low_ref.shape[1]
+    ahead_ref[:, :half] = (near_ref[:, :half].astype(F32) + low_ref[...].astype(F32)).astype(BF)
+    ahead_ref[:, half:] = near_ref[:, half:]
+    behind_ref[:, :half] = far_ref[:, :half]
+    behind_ref[:, half:] = (far_ref[:, half:].astype(F32) + high_ref[...].astype(F32)).astype(BF)
+
+
+def join(ahead, behind, low, high, dep):
+    return pl.pallas_call(
+        join_wide_kernel,
+        in_specs=[pl.BlockSpec(memory_space=pltpu.VMEM)] * 4 + [pl.BlockSpec(memory_space=pl.ANY)],
+        out_specs=[pl.BlockSpec(memory_space=pltpu.VMEM)] * 2,
+        out_shape=[jax.ShapeDtypeStruct(ahead.shape, BF)] * 2,
+        compiler_params=pltpu.CompilerParams(vmem_limit_bytes=VMEM_LIMIT),
+        cost_estimate=pl.CostEstimate(flops=1000, bytes_accessed=1000, transcendentals=0),
+    )(ahead, behind, low, high, dep)
 
 
 def pick_kernel(most, tile, base_ref, slot_ref, rows_ref, out_ref, acc):
@@ -235,7 +260,13 @@
     part_lower = lax.dot_general(
         activated, grad_out, (((0,), (0,)), ((), ())), preferred_element_type=F32
     ).astype(BF)
-    grad_lower = lax.psum_scatter(part_lower, "dp", scatter_dimension=0, tiled=True)
+    rows_l, half_w = ff // N_REP, width // 2
+    lower_term = [
+        lax.dynamic_slice_in_dim(part_lower, ((rep + d) % N_REP) * rows_l, rows_l, 0)
+        for d in range(N_REP)
+    ]
+    lower_low = along_y(lower_term[2][:, :half_w], 1)
+    lower_high = along_y(lower_term[2][:, half_w:], -1)
 
     pulled = lax.dot_general(
         cot_rows, lower, (((1,), (1,)), ((), ())), preferred_element_type=F32
@@ -245,7 +276,7 @@
     grad_hidden = (grad_act * lifted * logistic * (1.0 + hidden * (1.0 - logistic))).astype(BF)
     grad_lifted = (grad_act * swished).astype(BF)
 
-    gate_parts, upper_parts = grads(grad_hidden, grad_lifted, rows_in, (part_lower,))
+    gate_parts, upper_parts = grads(grad_hidden, grad_lifted, rows_in, ())
     grad_gate = lax.psum_scatter(gate_parts, "dp", scatter_dimension=0, tiled=True)
     grad_upper = lax.psum_scatter(upper_parts, "dp", scatter_dimension=0, tiled=True)
 
@@ -260,6 +291,11 @@
         (gate_parts, upper_parts),
     )
     came = lax.all_to_all(packed, "expert", split_axis=0, concat_axis=0, tiled=True)
+    ahead, behind = join(lower_term[1], lower_term[3], lower_low, lower_high, packed)
+    lower_got = along_y(ahead, 1), along_y(behind, -1)
+    grad_lower = (
+        lower_term[0].astype(F32) + lower_got[0].astype(F32) + lower_got[1].astype(F32)
+    ).astype(BF)
 
     named_any = jnp.any(named_here, axis=1)
     rank = jnp.where(named_any, running_count(named_any)[0] - 1, -1).T

time: 393 us -> 386 us (0.982)
  waiting for transfers between devices: 233 us -> 206 us
  local copies, waits for them, and re-layouts: 6.61 us -> 12.6 us
  starting transfers between devices: 14.6 us -> 19.8 us
    all_to_all x1, waiting for transfers between devices: 121 us -> 35.8 us  [local(): lax.all_to_all(packed, 'expert', split_axis=0, concat_axis=0, tiled=True)]
    ppermute x0 -> x4, waiting for transfers between devices: none -> 61.1 us  [along_y(): return lax.ppermute(v, 'dp', [(r, (r + by) % N_REP) for r in range(N_REP)])]
    ppermute x0 -> x4, starting transfers between devices: none -> 5.33 us  [along_y(): return lax.ppermute(v, 'dp', [(r, (r + by) % N_REP) for r in range(N_REP)])]
  transfers between devices with their start and end apart: 7 -> 10, of which waited for: 4 -> 7; matrix products, arithmetic and copies ran while one was open for 9% -> 13% of each run, Pallas kernels for 9% -> 11%
where the time goes in v2:
time: 386 us; the launch traced here: 385 us
  waiting for transfers between devices  206 us (53%)
  Pallas kernels  70.5 us (18%)
  matrix products  41.6 us (11%)
  starting transfers between devices  19.8 us (5%)
  between operations  15.2 us (4%)
  local copies, waits for them, and re-layouts  12.6 us (3%)
  other arithmetic  11 us (3%)
  blocking collectives  9.08 us (2%)
    ppermute x4, waiting for transfers between devices, along_y(): return lax.ppermute(v, 'dp', [(r, (r + by) % N_REP) for r in range(N_REP)])  61.1 us
    all_gather x1, waiting for transfers between devices, local(): dy_all = lax.all_gather(cotangent, 'expert', axis=0, tiled=True)  53.4 us
    all_gather x1, waiting for transfers between devices, local(): x_all = lax.all_gather(tokens, 'expert', axis=0, tiled=True)  50 us
    all_to_all x1, waiting for transfers between devices, local(): lax.all_to_all(packed, 'expert', split_axis=0, concat_axis=0, tiled=True)  35.8 us
    pallas_call x2, Pallas kernels, pick(): pl.pallas_call(functools.partial(pick_kernel, most, min(512, width)), gri...  30.3 us
    pallas_call x1, Pallas kernels, back_blocks(): pl.pallas_call(functools.partial(back_kernel, most_block, width), grid_sp...  21.8 us
    pallas_call x1, Pallas kernels, grads(): pl.pallas_call(grads_kernel, grid=(N_REP,), in_specs=[fixed, fixed, pl.Bl...  15 us
    dot_general x1, matrix products, local(): lax.dot_general(cot_rows, lower, (((1,), (1,)), ((), ())), preferred_elem...  11.6 us
  transfers between devices with their start and end apart: 10, of which 7 were waited for; matrix products, arithmetic and copies ran while one was open for 13% of the time, Pallas kernels for 11%

profile of v2, /device:TPU:32, one launch (start us, length us, event | category | flops | bytes accessed | tf_op | source)
XLA Modules:
  0.0 385.4 jit_solution(14561898255709156729)
XLA Ops:
  11.4 8.0 %all-to-all-start = ((bf16[32,1,128]{2,1,0:T(2,128)(2,1)}), bf16[32,1,128]{2,1,0:T(2,128)(2,1)S(1)}, u32[]{:S(2)}, u32[]{:S(2)}) async-start(bf16[32,1,128]{2,1,0:T(2,128)(2,1)} %copy.63), calls=%async_computation | async-start | bytes 32768 | tf_op jit(solution)/shard_map/all_to_all | solution.py:242
  22.0 3.5 all-to-all-done
  28.2 9.1 %all-reduce = s32[4]{0:T(128)S(1)} all-reduce(s32[4]{0:T(128)S(1)} %dynamic-update-slice), channel_id=2, replica_groups=mesh['dp'=4,'expert'=32] {'dp'}, use_global_device_ids=true, to_apply=%add | all-reduce | flops 4 | bytes 32
  41.1 2.5 fusion.12
  44.1 50.0 %all-gather.5.cloned.1.call-done.rows_ref = bf16[4096,2560]{1,0:T(8,128)(2,1)} async-done(((bf16[128,2560]{1,0:T(8,128)(2,1)}), bf16[4096,2560]{1,0:T(8,128)(2,1)}) %all-gather.5.cloned.1.call-update) | async-done | bytes 20971536 | tf_op jit(solution)/shard_map/all_gather | solution.py:244
  94.1 15.4 %shard_map.120.rows_ref = bf16[864,2560]{1,0:T(8,128)(2,1)} custom-call(s32[8]{0:T(128)} %fusion.19.base_ref, s32[8,1,512]{2,1,0:T(1,128)} %bitcast.65, bf16[4096,2560]{1,0:T(8,128)(2,1)} %all-gather.5.cloned.1.call-done.rows_ref), custom_call_target="tpu_custom_call" | custom-call | flops 4362076160 | bytes 25395200 | tf_op jit(solution)/shard_map/pallas_call | solution.py:72
  109.5 8.9 %fusion.5 = f32[864,832]{1,0:T(8,128)} fusion(bf16[864,2560]{1,0:T(8,128)(2,1)} %shard_map.120.rows_ref, bf16[1,2560,832]{1,2,0:T(8,128)(2,1)S(1)} %bitcast.60), kind=kOutput, calls=%fused_computation.8 | convolution fusion | flops 3680501760 | bytes 11558912 | tf_op jit(solution)/shard_map/dot_general | solution.py:254
  118.4 6.5 %fusion.3 = f32[864,832]{1,0:T(8,128)} fusion(bf16[864,2560]{1,0:T(8,128)(2,1)S(1)} %copy-done, bf16[1,2560,832]{1,2,0:T(8,128)(2,1)S(1)} %bitcast.63), kind=kOutput, calls=%fused_computation.6 | convolution fusion | flops 3680501760 | bytes 11558912 | tf_op jit(solution)/shard_map/dot_general | solution.py:253
  124.8 53.4 %all-gather.3.cloned.1.call-done.rows_ref = bf16[4096,2560]{1,0:T(8,128)(2,1)} async-done(((bf16[128,2560]{1,0:T(8,128)(2,1)}), bf16[4096,2560]{1,0:T(8,128)(2,1)}) %all-gather.3.cloned.1.call-update) | async-done | bytes 20971536 | tf_op jit(solution)/shard_map/all_gather | solution.py:245
  178.2 14.9 %shard_map.119 = bf16[864,2560]{1,0:T(8,128)(2,1)} custom-call(s32[8]{0:T(128)} %fusion.19.base_ref, s32[8,1,512]{2,1,0:T(1,128)} %bitcast.66, bf16[4096,2560]{1,0:T(8,128)(2,1)} %all-gather.3.cloned.1.call-done.rows_ref), custom_call_target="tpu_custom_call" | custom-call | flops 4362076160 | bytes 25395200 | tf_op jit(solution)/shard_map/pallas_call | solution.py:72
  193.1 11.6 %multiply_reduce_fusion = (f32[864]{0:T(1024)S(1)}, bf16[864,832]{1,0:T(8,128)(2,1)S(1)}, bf16[864,832]{1,0:T(8,128)(2,1)}, bf16[864,832]{1,0:T(8,128)(2,1)}) fusion(f32[864,832]{1,0:T(8,128)S(1)} %copy-done.7, f32[864,832]{1,0:T(8,128)} %fusion.3, f32[864]{0:T(1024)S(1)} %fusion.12, bf16[864,2560]{1,0:T(8,128)(2,1)} %shard_map.119, ...), kind=kOutput, calls=%fused_computation.13 | convolution fusion | flops 3694159104 | bytes 18754304 | tf_op jit(solution)/shard_map/dot_general | solution.py:271
  204.7 15.0 %shard_map.121 = (bf16[3328,640]{1,0:T(8,128)(2,1)}, bf16[3328,640]{1,0:T(8,128)(2,1)}) custom-call(bf16[864,832]{1,0:T(8,128)(2,1)} %get-tuple-element.19.hidden_ref, bf16[864,832]{1,0:T(8,128)(2,1)} %get-tuple-element.20.lifted_ref, bf16[864,2560]{1,0:T(8,128)(2,1)} %shard_map.120.rows_ref), custom_call_target="tpu_custom_call" | custom-call | flops 7361003520 | bytes 12943360 | tf_op jit(solution)/shard_map/pallas_call | solution.py:176
  220.7 21.8 %shard_map.122.dep_ref = bf16[32,48,2688]{2,1,0:T(8,128)(2,1)} custom-call(s32[32]{0:T(128)} %get-tuple-element.14.first_ref, bf16[864,832]{1,0:T(8,128)(2,1)} %get-tuple-element.19.hidden_ref, bf16[864,832]{1,0:T(8,128)(2,1)} %get-tuple-element.20.lifted_ref, bf16[832,2560]{1,0:T(8,128)(2,1)} %bitcast.61, bf16[832,2560]{1,0:T(8,128)(2,1)} %bitcast.58, ...), custom_call_target="tpu_custom_call" | custom-call | flops 7361003520 | bytes 24248320 | tf_op jit(solution)/shard_map/pallas_call | solution.py:138
  242.5 6.3 %all-to-all-start.1 = ((bf16[32,48,2688]{2,1,0:T(8,128)(2,1)}), bf16[32,48,2688]{2,1,0:T(8,128)(2,1)}, u32[]{:S(2)}, u32[]{:S(2)}) async-start(bf16[32,48,2688]{2,1,0:T(8,128)(2,1)} %shard_map.122.dep_ref), calls=%async_computation.1 | async-start | bytes 16515072 | tf_op jit(solution)/shard_map/all_to_all | solution.py:293
  249.4 7.2 %convolution_convert_fusion = bf16[832,2560]{1,0:T(8,128)(2,1)S(1)} fusion(bf16[864,832]{1,0:T(8,128)(2,1)S(1)} %get-tuple-element.16, bf16[864,2560]{1,0:T(8,128)(2,1)} %shard_map.119, f32[864]{0:T(1024)S(1)} %fusion.12), kind=kOutput, calls=%fused_computation.4 | convolution fusion | flops 3689267200 | bytes 10124672 | tf_op jit(solution)/shard_map/dot_general | solution.py:260
  256.6 2.0 copy-done.1
  261.9 3.1 constant_dynamic-slice_fusion.1
  265.0 12.3 %collective-permute-done.low_ref = bf16[208,1280]{1,0:T(8,128)(2,1)S(1)} collective-permute-done((bf16[208,1280]{1,0:T(8,128)(2,1)S(1)}, bf16[208,1280]{1,0:T(8,128)(2,1)S(1)}, u32[]{:S(2)}, u32[]{:S(2)}) %collective-permute-start) | collective-permute-done | bytes 532512 | tf_op jit(solution)/shard_map/ppermute | solution.py:20
  278.3 3.4 shard_map.123
  283.9 46.8 %collective-permute-done.3 = bf16[208,2560]{1,0:T(8,128)(2,1)S(1)} collective-permute-done((bf16[208,2560]{1,0:T(8,128)(2,1)}, bf16[208,2560]{1,0:T(8,128)(2,1)S(1)}, u32[]{:S(2)}, u32[]{:S(2)}) %collective-permute-start.3) | collective-permute-done | bytes 1064992 | tf_op jit(solution)/shard_map/ppermute | solution.py:20
  330.7 2.0 collective-permute-done.2
  332.7 2.6 fusion.13
  335.3 35.8 %all-to-all-done.1 = bf16[32,48,2688]{2,1,0:T(8,128)(2,1)} async-done(((bf16[32,48,2688]{2,1,0:T(8,128)(2,1)}), bf16[32,48,2688]{2,1,0:T(8,128)(2,1)}, u32[]{:S(2)}, u32[]{:S(2)}) %all-to-all-start.1) | async-done | bytes 8257568 | tf_op jit(solution)/shard_map/all_to_all | solution.py:293
  371.0 4.7 %convolution_bitcast_fusion = bf16[128,2688]{1,0:T(8,128)(2,1)S(1)} fusion(bf16[32,48,2688]{2,1,0:T(8,128)(2,1)} %all-to-all-done.1, s32[128,32]{0,1:T(8,128)S(1)} %fusion.11), kind=kOutput, calls=%fused_computation.12 | convolution fusion | flops 1057161216 | bytes 8962048 | tf_op jit(solution)/shard_map/dot_general | solution.py:303
  (68 shorter events, 23.6 us)
Async XLA Ops:
  7.2 86.9 %all-gather.5.cloned.1.call-start = ((), (), s32[]{:S(2)}) async-start(), calls=%async_computation.5 | async-start | bytes 21626880 | tf_op jit(solution)/shard_map/all_gather | solution.py:244
  7.9 170.3 %all-gather.3.cloned.1.call-start = ((), (), s32[]{:S(2)}) async-start(), calls=%async_computation.4 | async-start | bytes 21626880 | tf_op jit(solution)/shard_map/all_gather | solution.py:245
  11.4 14.1 %all-to-all-start = ((bf16[32,1,128]{2,1,0:T(2,128)(2,1)}), bf16[32,1,128]{2,1,0:T(2,128)(2,1)S(1)}, u32[]{:S(2)}, u32[]{:S(2)}) async-start(bf16[32,1,128]{2,1,0:T(2,128)(2,1)} %copy.63), calls=%async_computation | async-start | bytes 32768 | tf_op jit(solution)/shard_map/all_to_all | solution.py:242
  19.4 359.4 %reduce-scatter.3.cloned.1.call-start = ((), (), s32[]{:S(2)}) async-start(), calls=%async_computation.6 | async-start | bytes 5324800 | tf_op jit(solution)/shard_map/reduce_scatter | solution.py:280
  41.1 53.0 %copy-start.4 = (s32[32,128]{1,0:T(8,128)}, s32[32,128]{1,0:T(8,128)S(1)}, u32[]{:S(2)}) copy-start(s32[32,128]{1,0:T(8,128)S(1)} %fusion.18) | copy-start | bytes 49156
  41.1 68.4 %slice-start = ((s8[4259840]{0:T(1024)(128)(4,1)}), s8[65536]{0:T(1024)(128)(4,1)S(1)}, s32[]{:S(2)}) async-start(s8[4259840]{0:T(1024)(128)(4,1)} %bitcast.59), calls=%async_computation.8 | async-start | bytes 131072
  94.1 15.4 %slice-start.1 = ((s8[4259840]{0:T(1024)(128)(4,1)}), s8[4194304]{0:T(1024)(128)(4,1)S(1)}, s32[]{:S(2)}) async-start(s8[4259840]{0:T(1024)(128)(4,1)} %bitcast.59), calls=%async_computation.9 | async-start | bytes 8388608
  94.1 24.3 %slice-start.2 = ((s8[4259840]{0:T(1024)(128)(4,1)}), s8[65536]{0:T(1024)(128)(4,1)S(1)}, s32[]{:S(2)}) async-start(s8[4259840]{0:T(1024)(128)(4,1)} %bitcast.62), calls=%async_computation.10 | async-start | bytes 131072
  109.5 8.9 %copy-start = (bf16[864,2560]{1,0:T(8,128)(2,1)S(1)}, bf16[864,2560]{1,0:T(8,128)(2,1)}, u32[]{:S(2)}) copy-start(bf16[864,2560]{1,0:T(8,128)(2,1)} %shard_map.120.rows_ref) | copy-start | bytes 13271044
  109.5 8.9 %slice-start.3 = ((s8[4259840]{0:T(1024)(128)(4,1)}), s8[4194304]{0:T(1024)(128)(4,1)S(1)}, s32[]{:S(2)}) async-start(s8[4259840]{0:T(1024)(128)(4,1)} %bitcast.62), calls=%async_computation.11 | async-start | bytes 8388608
  178.2 14.9 %copy-start.7 = (f32[864,832]{1,0:T(8,128)S(1)}, f32[864,832]{1,0:T(8,128)}, u32[]{:S(2)}) copy-start(f32[864,832]{1,0:T(8,128)} %fusion.5) | copy-start | bytes 8626180
  242.5 128.6 %all-to-all-start.1 = ((bf16[32,48,2688]{2,1,0:T(8,128)(2,1)}), bf16[32,48,2688]{2,1,0:T(8,128)(2,1)}, u32[]{:S(2)}, u32[]{:S(2)}) async-start(bf16[32,48,2688]{2,1,0:T(8,128)(2,1)} %shard_map.122.dep_ref), calls=%async_computation.1 | async-start | bytes 16515072 | tf_op jit(solution)/shard_map/all_to_all | solution.py:293
  248.8 130.1 %reduce-scatter.5.cloned.1.call-start = ((), (), s32[]{:S(2)}) async-start(), calls=%async_computation.7 | async-start | bytes 5324800 | tf_op jit(solution)/shard_map/reduce_scatter | solution.py:281
  256.6 2.0 copy-start.1
  258.6 18.7 %collective-permute-start = (bf16[208,1280]{1,0:T(8,128)(2,1)S(1)}, bf16[208,1280]{1,0:T(8,128)(2,1)S(1)}, u32[]{:S(2)}, u32[]{:S(2)}) collective-permute-start(bf16[208,1280]{1,0:T(8,128)(2,1)S(1)} %get-tuple-element.22), channel_id=1, source_target_pairs={{0,32},{32,64},{64,96},{96,0},{1,33},{33,65},{65,97},{97,1},{2,34}... | collective-permute-start | bytes 1597448 | tf_op jit(solution)/shard_map/ppermute | solution.py:20
  260.1 17.2 %collective-permute-start.1 = (bf16[208,1280]{1,0:T(8,128)(2,1)S(1)}, bf16[208,1280]{1,0:T(8,128)(2,1)S(1)}, u32[]{:S(2)}, u32[]{:S(2)}) collective-permute-start(bf16[208,1280]{1,0:T(8,128)(2,1)S(1)} %get-tuple-element.21), channel_id=1, source_target_pairs={{0,96},{32,0},{64,32},{96,64},{1,97},{33,1},{65,33},{97,65},{2,98}... | collective-permute-start | bytes 1597448 | tf_op jit(solution)/shard_map/ppermute | solution.py:20
  277.3 0.8 copy-start.2
  277.3 1.0 copy-start.3
  278.3 5.4 %copy-start.6 = (s32[128,6]{0,1:T(8,128)S(1)}, s32[128,6]{0,1:T(8,128)}, u32[]{:S(2)}) copy-start(s32[128,6]{0,1:T(8,128)} %param.10) | copy-start | bytes 9220
  281.7 49.0 %collective-permute-start.3 = (bf16[208,2560]{1,0:T(8,128)(2,1)}, bf16[208,2560]{1,0:T(8,128)(2,1)S(1)}, u32[]{:S(2)}, u32[]{:S(2)}) collective-permute-start(bf16[208,2560]{1,0:T(8,128)(2,1)} %get-tuple-element.12), channel_id=1, source_target_pairs={{0,96},{32,0},{64,32},{96,64},{1,97},{33,1},{65,33},{97,65},{2,98}... | collective-permute-start | bytes 3194888 | tf_op jit(solution)/shard_map/ppermute | solution.py:20
  282.5 50.2 %collective-permute-start.2 = (bf16[208,2560]{1,0:T(8,128)(2,1)}, bf16[208,2560]{1,0:T(8,128)(2,1)S(1)}, u32[]{:S(2)}, u32[]{:S(2)}) collective-permute-start(bf16[208,2560]{1,0:T(8,128)(2,1)} %get-tuple-element.11), channel_id=1, source_target_pairs={{0,32},{32,64},{64,96},{96,0},{1,33},{33,65},{65,97},{97,1},{2,34}... | collective-permute-start | bytes 3194888 | tf_op jit(solution)/shard_map/ppermute | solution.py:20
  335.3 43.0 %copy-start.5 = (f32[128,6]{0,1:T(8,128)S(1)}, f32[128,6]{0,1:T(8,128)}, u32[]{:S(2)}) copy-start(f32[128,6]{0,1:T(8,128)} %param.11) | copy-start | bytes 9220
Sparse Core Ops, SparseCore 0:
  10.2 83.8 all-gather.4
  96.4 81.7 all-gather.2
  219.9 50.5 reduce-scatter.2
  273.4 69.0 reduce-scatter.4

commit v3 on v2

--- a/solution.py
+++ b/solution.py
@@ -89,6 +89,43 @@
             transcendentals=0,
         ),
     )(base, slot.reshape(groups, 1, blocks * count), rows)
+
+
+def inner_kernel(cot_ref, lower_ref, hidden_ref, lifted_ref, act_ref, scale_ref, out_h, out_l, share):
+    pulled = lax.dot_general(
+        cot_ref[...], lower_ref[...], (((1,), (1,)), ((), ())), preferred_element_type=F32
+    )
+    hidden = hidden_ref[...]
+    logistic = jax.nn.sigmoid(hidden)
+    share[...] = jnp.sum(act_ref[...].astype(F32) * pulled, axis=1, keepdims=True)
+    grad_act = scale_ref[...] * pulled
+    out_h[...] = (
+        grad_act * lifted_ref[...] * logistic * (1.0 + hidden * (1.0 - logistic))
+    ).astype(BF)
+    out_l[...] = (grad_act * (hidden * logistic)).astype(BF)
+
+
+def inner_grads(cot_rows, lower, hidden, lifted, activated, row_scale):
+    slots, ff = hidden.shape
+    step = slots // 3
+    wide = pl.BlockSpec((step, ff), lambda m: (m, 0))
+    one = pl.BlockSpec((step, 1), lambda m: (m, 0))
+    return pl.pallas_call(
+        inner_kernel,
+        grid=(3,),
+        in_specs=[
+            pl.BlockSpec((step, lower.shape[1]), lambda m: (m, 0)),
+            pl.BlockSpec(lower.shape, lambda m: (0, 0)),
+            wide,
+            wide,
+            wide,
+            one,
+        ],
+        out_specs=[wide, wide, one],
+        out_shape=[jax.ShapeDtypeStruct((slots, ff), BF)] * 2
+        + [jax.ShapeDtypeStruct((slots, 1), F32)],
+        compiler_params=pltpu.CompilerParams(vmem_limit_bytes=VMEM_LIMIT),
+    )(cot_rows, lower, hidden, lifted, activated, row_scale)
 
 
 def back_kernel(
@@ -268,13 +305,10 @@
     lower_low = along_y(lower_term[2][:, :half_w], 1)
     lower_high = along_y(lower_term[2][:, half_w:], -1)
 
-    pulled = lax.dot_general(
-        cot_rows, lower, (((1,), (1,)), ((), ())), preferred_element_type=F32
-    )
-    shares = jnp.sum(activated.astype(F32) * pulled, axis=1)
-    grad_act = row_scale * pulled
-    grad_hidden = (grad_act * lifted * logistic * (1.0 + hidden * (1.0 - logistic))).astype(BF)
-    grad_lifted = (grad_act * swished).astype(BF)
+    grad_hidden, grad_lifted, shares = inner_grads(
+        cot_rows, lower, hidden, lifted, activated, row_scale
+    )
+    shares = shares[:, 0]
 
     gate_parts, upper_parts = grads(grad_hidden, grad_lifted, rows_in, ())
     grad_gate = lax.psum_scatter(gate_parts, "dp", scatter_dimension=0, tiled=True)

time: 386 us -> 385 us (level)
  matrix products: 41.6 us -> 28 us
  Pallas kernels: 70.5 us -> 81.8 us
    pallas_call x0 -> x1, Pallas kernels: none -> 11.6 us  [inner_grads(): pl.pallas_call(inner_kernel, grid=(3,), in_specs=[pl.BlockSpec((step, low...]
    dot_general x1 -> x0, matrix products: 11.6 us -> none  [local(): lax.dot_general(cot_rows, lower, (((1,), (1,)), ((), ())), preferred_elem...]
where the time goes in v3:
time: 385 us; the launch traced here: 384 us
  waiting for transfers between devices  206 us (54%)
  Pallas kernels  81.8 us (21%)
  matrix products  28 us (7%)
  starting transfers between devices  20.1 us (5%)
  between operations  15.3 us (4%)
  local copies, waits for them, and re-layouts  13.4 us (3%)
  other arithmetic  11 us (3%)
  blocking collectives  9.09 us (2%)
    ppermute x4, waiting for transfers between devices, along_y(): return lax.ppermute(v, 'dp', [(r, (r + by) % N_REP) for r in range(N_REP)])  61.2 us
    all_gather x1, waiting for transfers between devices, local(): dy_all = lax.all_gather(cotangent, 'expert', axis=0, tiled=True)  55.3 us
    all_gather x1, waiting for transfers between devices, local(): x_all = lax.all_gather(tokens, 'expert', axis=0, tiled=True)  49.1 us
    all_to_all x1, waiting for transfers between devices, local(): lax.all_to_all(packed, 'expert', split_axis=0, concat_axis=0, tiled=True)  34.9 us
    pallas_call x2, Pallas kernels, pick(): pl.pallas_call(functools.partial(pick_kernel, most, min(512, width)), gri...  30 us
    pallas_call x1, Pallas kernels, back_blocks(): pl.pallas_call(functools.partial(back_kernel, most_block, width), grid_sp...  21.8 us
    pallas_call x1, Pallas kernels, grads(): pl.pallas_call(grads_kernel, grid=(N_REP,), in_specs=[fixed, fixed, pl.Bl...  15 us
    pallas_call x1, Pallas kernels, inner_grads(): pl.pallas_call(inner_kernel, grid=(3,), in_specs=[pl.BlockSpec((step, low...  11.6 us
  transfers between devices with their start and end apart: 10, of which 7 were waited for; matrix products, arithmetic and copies ran while one was open for 13% of the time, Pallas kernels for 11%

profile of v3, /device:TPU:32, one launch (start us, length us, event | category | flops | bytes accessed | tf_op | source)
XLA Modules:
  0.0 384.3 jit_solution(666875703338269068)
XLA Ops:
  11.4 8.0 %all-to-all-start = ((bf16[32,1,128]{2,1,0:T(2,128)(2,1)}), bf16[32,1,128]{2,1,0:T(2,128)(2,1)S(1)}, u32[]{:S(2)}, u32[]{:S(2)}) async-start(bf16[32,1,128]{2,1,0:T(2,128)(2,1)} %copy.53), calls=%async_computation | async-start | bytes 32768 | tf_op jit(solution)/shard_map/all_to_all | solution.py:279
  22.0 3.5 all-to-all-done
  28.2 9.1 %all-reduce = s32[4]{0:T(128)S(1)} all-reduce(s32[4]{0:T(128)S(1)} %dynamic-update-slice), channel_id=2, replica_groups=mesh['dp'=4,'expert'=32] {'dp'}, use_global_device_ids=true, to_apply=%add | all-reduce | flops 4 | bytes 32
  41.0 2.5 fusion.9
  45.1 49.1 %all-gather.5.cloned.1.call-done.rows_ref = bf16[4096,2560]{1,0:T(8,128)(2,1)} async-done(((bf16[128,2560]{1,0:T(8,128)(2,1)}), bf16[4096,2560]{1,0:T(8,128)(2,1)}) %all-gather.5.cloned.1.call-update) | async-done | bytes 20971536 | tf_op jit(solution)/shard_map/all_gather | solution.py:281
  94.1 15.4 %shard_map.120.rows_ref = bf16[864,2560]{1,0:T(8,128)(2,1)} custom-call(s32[8]{0:T(128)} %fusion.16.base_ref, s32[8,1,512]{2,1,0:T(1,128)} %bitcast.63, bf16[4096,2560]{1,0:T(8,128)(2,1)} %all-gather.5.cloned.1.call-done.rows_ref), custom_call_target="tpu_custom_call" | custom-call | flops 4362076160 | bytes 25395200 | tf_op jit(solution)/shard_map/pallas_call | solution.py:72
  109.5 6.9 %fusion.5.hidden_ref = f32[864,832]{1,0:T(8,128)S(1)} fusion(bf16[864,2560]{1,0:T(8,128)(2,1)} %shard_map.120.rows_ref, bf16[1,2560,832]{1,2,0:T(8,128)(2,1)S(1)} %bitcast.58), kind=kOutput, calls=%fused_computation.8 | convolution fusion | flops 3680501760 | bytes 11558912 | tf_op jit(solution)/shard_map/dot_general | solution.py:290
  116.5 6.5 %multiply_convert_fusion.2 = (bf16[864,832]{1,0:T(8,128)(2,1)}, f32[864,832]{1,0:T(8,128)}) fusion(f32[864,832]{1,0:T(8,128)S(1)} %fusion.5.hidden_ref, bf16[864,2560]{1,0:T(8,128)(2,1)S(1)} %copy-done, bf16[1,2560,832]{1,2,0:T(8,128)(2,1)S(1)} %bitcast.61), kind=kOutput, calls=%fused_computation.11 | convolution fusion | flops 3684814848 | bytes 15872000 | tf_op jit(solution)/shard_map/dot_general | solution.py:291
  123.0 55.3 %all-gather.3.cloned.1.call-done.rows_ref = bf16[4096,2560]{1,0:T(8,128)(2,1)} async-done(((bf16[128,2560]{1,0:T(8,128)(2,1)}), bf16[4096,2560]{1,0:T(8,128)(2,1)}) %all-gather.3.cloned.1.call-update) | async-done | bytes 20971536 | tf_op jit(solution)/shard_map/all_gather | solution.py:282
  178.2 14.7 %shard_map.119.cot_ref = bf16[864,2560]{1,0:T(8,128)(2,1)} custom-call(s32[8]{0:T(128)} %fusion.16.base_ref, s32[8,1,512]{2,1,0:T(1,128)} %bitcast.64, bf16[4096,2560]{1,0:T(8,128)(2,1)} %all-gather.3.cloned.1.call-done.rows_ref), custom_call_target="tpu_custom_call" | custom-call | flops 4362076160 | bytes 25395200 | tf_op jit(solution)/shard_map/pallas_call | solution.py:72
  192.9 11.6 %shard_map.121 = (bf16[864,832]{1,0:T(8,128)(2,1)}, bf16[864,832]{1,0:T(8,128)(2,1)}, f32[864,1]{1,0:T(8,128)}) custom-call(bf16[864,2560]{1,0:T(8,128)(2,1)} %shard_map.119.cot_ref, bf16[832,2560]{1,0:T(8,128)(2,1)} %bitcast.55, f32[864,832]{1,0:T(8,128)} %copy-done.2, f32[864,832]{1,0:T(8,128)} %get-tuple-element.28.lifted_ref, ...), custom_call_target="tpu_custom_call" | custom-call | tf_op jit(solution)/shard_map/pallas_call | solution.py:113
  204.5 15.0 %shard_map.122 = (bf16[3328,640]{1,0:T(8,128)(2,1)}, bf16[3328,640]{1,0:T(8,128)(2,1)}) custom-call(bf16[864,832]{1,0:T(8,128)(2,1)} %get-tuple-element.12.hidden_ref, bf16[864,832]{1,0:T(8,128)(2,1)} %get-tuple-element.13.lifted_ref, bf16[864,2560]{1,0:T(8,128)(2,1)} %shard_map.120.rows_ref), custom_call_target="tpu_custom_call" | custom-call | flops 7361003520 | bytes 12943360 | tf_op jit(solution)/shard_map/pallas_call | solution.py:213
  219.5 21.8 %shard_map.123.dep_ref = bf16[32,48,2688]{2,1,0:T(8,128)(2,1)} custom-call(s32[32]{0:T(128)} %get-tuple-element.20.first_ref, bf16[864,832]{1,0:T(8,128)(2,1)} %get-tuple-element.12.hidden_ref, bf16[864,832]{1,0:T(8,128)(2,1)} %get-tuple-element.13.lifted_ref, bf16[832,2560]{1,0:T(8,128)(2,1)} %bitcast.56, bf16[832,2560]{1,0:T(8,128)(2,1)} %bitcast.59, ...), custom_call_target="tpu_custom_call" | custom-call | flops 7361003520 | bytes 24248320 | tf_op jit(solution)/shard_map/pallas_call | solution.py:175
  241.3 6.3 %all-to-all-start.1 = ((bf16[32,48,2688]{2,1,0:T(8,128)(2,1)}), bf16[32,48,2688]{2,1,0:T(8,128)(2,1)}, u32[]{:S(2)}, u32[]{:S(2)}) async-start(bf16[32,48,2688]{2,1,0:T(8,128)(2,1)} %shard_map.123.dep_ref), calls=%async_computation.1 | async-start | bytes 16515072 | tf_op jit(solution)/shard_map/all_to_all | solution.py:327
  249.1 7.2 %convolution_convert_fusion = bf16[832,2560]{1,0:T(8,128)(2,1)S(1)} fusion(bf16[864,832]{1,0:T(8,128)(2,1)S(1)} %copy-done.3, bf16[864,2560]{1,0:T(8,128)(2,1)} %shard_map.119.cot_ref, f32[864]{0:T(1024)S(1)} %fusion.9), kind=kOutput, calls=%fused_computation.4 | convolution fusion | flops 3689267200 | bytes 10124672 | tf_op jit(solution)/shard_map/dot_general | solution.py:297
  256.3 2.0 copy-done.1
  261.6 3.1 constant_dynamic-slice_fusion.1
  264.7 12.5 %collective-permute-done.low_ref = bf16[208,1280]{1,0:T(8,128)(2,1)S(1)} collective-permute-done((bf16[208,1280]{1,0:T(8,128)(2,1)S(1)}, bf16[208,1280]{1,0:T(8,128)(2,1)S(1)}, u32[]{:S(2)}, u32[]{:S(2)}) %collective-permute-start) | collective-permute-done | bytes 532512 | tf_op jit(solution)/shard_map/ppermute | solution.py:20
  278.1 3.4 shard_map.124
  283.7 46.8 %collective-permute-done.3 = bf16[208,2560]{1,0:T(8,128)(2,1)S(1)} collective-permute-done((bf16[208,2560]{1,0:T(8,128)(2,1)}, bf16[208,2560]{1,0:T(8,128)(2,1)S(1)}, u32[]{:S(2)}, u32[]{:S(2)}) %collective-permute-start.3) | collective-permute-done | bytes 1064992 | tf_op jit(solution)/shard_map/ppermute | solution.py:20
  330.5 2.0 collective-permute-done.2
  332.5 2.6 fusion.10
  335.1 34.9 %all-to-all-done.1 = bf16[32,48,2688]{2,1,0:T(8,128)(2,1)} async-done(((bf16[32,48,2688]{2,1,0:T(8,128)(2,1)}), bf16[32,48,2688]{2,1,0:T(8,128)(2,1)}, u32[]{:S(2)}, u32[]{:S(2)}) %all-to-all-start.1) | async-done | bytes 8257568 | tf_op jit(solution)/shard_map/all_to_all | solution.py:327
  369.9 4.7 %convolution_bitcast_fusion = bf16[128,2688]{1,0:T(8,128)(2,1)S(1)} fusion(bf16[32,48,2688]{2,1,0:T(8,128)(2,1)} %all-to-all-done.1, s32[128,32]{0,1:T(8,128)S(1)} %fusion.8), kind=kOutput, calls=%fused_computation.10 | convolution fusion | flops 1057161216 | bytes 8962048 | tf_op jit(solution)/shard_map/dot_general | solution.py:337
  (70 shorter events, 24.4 us)
Async XLA Ops:
  7.2 87.0 %all-gather.5.cloned.1.call-start = ((), (), s32[]{:S(2)}) async-start(), calls=%async_computation.5 | async-start | bytes 21626880 | tf_op jit(solution)/shard_map/all_gather | solution.py:281
  7.9 170.3 %all-gather.3.cloned.1.call-start = ((), (), s32[]{:S(2)}) async-start(), calls=%async_computation.4 | async-start | bytes 21626880 | tf_op jit(solution)/shard_map/all_gather | solution.py:282
  11.4 14.1 %all-to-all-start = ((bf16[32,1,128]{2,1,0:T(2,128)(2,1)}), bf16[32,1,128]{2,1,0:T(2,128)(2,1)S(1)}, u32[]{:S(2)}, u32[]{:S(2)}) async-start(bf16[32,1,128]{2,1,0:T(2,128)(2,1)} %copy.53), calls=%async_computation | async-start | bytes 32768 | tf_op jit(solution)/shard_map/all_to_all | solution.py:279
  19.4 358.4 %reduce-scatter.3.cloned.1.call-start = ((), (), s32[]{:S(2)}) async-start(), calls=%async_computation.6 | async-start | bytes 5324800 | tf_op jit(solution)/shard_map/reduce_scatter | solution.py:314
  41.0 53.1 %copy-start.6 = (s32[32,128]{1,0:T(8,128)}, s32[32,128]{1,0:T(8,128)S(1)}, u32[]{:S(2)}) copy-start(s32[32,128]{1,0:T(8,128)S(1)} %fusion.15) | copy-start | bytes 49156
  43.5 66.0 %slice-start = ((s8[4259840]{0:T(1024)(128)(4,1)}), s8[65536]{0:T(1024)(128)(4,1)S(1)}, s32[]{:S(2)}) async-start(s8[4259840]{0:T(1024)(128)(4,1)} %bitcast.57), calls=%async_computation.8 | async-start | bytes 131072
  94.1 15.4 %slice-start.1 = ((s8[4259840]{0:T(1024)(128)(4,1)}), s8[4194304]{0:T(1024)(128)(4,1)S(1)}, s32[]{:S(2)}) async-start(s8[4259840]{0:T(1024)(128)(4,1)} %bitcast.57), calls=%async_computation.9 | async-start | bytes 8388608
  94.1 22.3 %slice-start.2 = ((s8[4259840]{0:T(1024)(128)(4,1)}), s8[65536]{0:T(1024)(128)(4,1)S(1)}, s32[]{:S(2)}) async-start(s8[4259840]{0:T(1024)(128)(4,1)} %bitcast.60), calls=%async_computation.10 | async-start | bytes 131072
  109.5 7.0 %copy-start = (bf16[864,2560]{1,0:T(8,128)(2,1)S(1)}, bf16[864,2560]{1,0:T(8,128)(2,1)}, u32[]{:S(2)}) copy-start(bf16[864,2560]{1,0:T(8,128)(2,1)} %shard_map.120.rows_ref) | copy-start | bytes 13271044
  109.5 7.0 %slice-start.3 = ((s8[4259840]{0:T(1024)(128)(4,1)}), s8[4194304]{0:T(1024)(128)(4,1)S(1)}, s32[]{:S(2)}) async-start(s8[4259840]{0:T(1024)(128)(4,1)} %bitcast.60), calls=%async_computation.11 | async-start | bytes 8388608
  116.5 6.5 %copy-start.2 = (f32[864,832]{1,0:T(8,128)}, f32[864,832]{1,0:T(8,128)S(1)}, u32[]{:S(2)}) copy-start(f32[864,832]{1,0:T(8,128)S(1)} %fusion.5.hidden_ref) | copy-start | bytes 8626180
  241.3 128.6 %all-to-all-start.1 = ((bf16[32,48,2688]{2,1,0:T(8,128)(2,1)}), bf16[32,48,2688]{2,1,0:T(8,128)(2,1)}, u32[]{:S(2)}, u32[]{:S(2)}) async-start(bf16[32,48,2688]{2,1,0:T(8,128)(2,1)} %shard_map.123.dep_ref), calls=%async_computation.1 | async-start | bytes 16515072 | tf_op jit(solution)/shard_map/all_to_all | solution.py:327
  247.7 1.4 copy-start.3
  247.7 130.1 %reduce-scatter.5.cloned.1.call-start = ((), (), s32[]{:S(2)}) async-start(), calls=%async_computation.7 | async-start | bytes 5324800 | tf_op jit(solution)/shard_map/reduce_scatter | solution.py:315
  256.2 2.0 copy-start.1
  258.3 18.8 %collective-permute-start = (bf16[208,1280]{1,0:T(8,128)(2,1)S(1)}, bf16[208,1280]{1,0:T(8,128)(2,1)S(1)}, u32[]{:S(2)}, u32[]{:S(2)}) collective-permute-start(bf16[208,1280]{1,0:T(8,128)(2,1)S(1)} %get-tuple-element.24), channel_id=1, source_target_pairs={{0,32},{32,64},{64,96},{96,0},{1,33},{33,65},{65,97},{97,1},{2,34}... | collective-permute-start | bytes 1597448 | tf_op jit(solution)/shard_map/ppermute | solution.py:20
  259.8 17.4 %collective-permute-start.1 = (bf16[208,1280]{1,0:T(8,128)(2,1)S(1)}, bf16[208,1280]{1,0:T(8,128)(2,1)S(1)}, u32[]{:S(2)}, u32[]{:S(2)}) collective-permute-start(bf16[208,1280]{1,0:T(8,128)(2,1)S(1)} %get-tuple-element.23), channel_id=1, source_target_pairs={{0,96},{32,0},{64,32},{96,64},{1,97},{33,1},{65,33},{97,65},{2,98}... | collective-permute-start | bytes 1597448 | tf_op jit(solution)/shard_map/ppermute | solution.py:20
  277.1 0.8 copy-start.4
  277.1 1.0 copy-start.5
  278.1 5.4 %copy-start.8 = (s32[128,6]{0,1:T(8,128)S(1)}, s32[128,6]{0,1:T(8,128)}, u32[]{:S(2)}) copy-start(s32[128,6]{0,1:T(8,128)} %param.10) | copy-start | bytes 9220
  281.5 49.0 %collective-permute-start.3 = (bf16[208,2560]{1,0:T(8,128)(2,1)}, bf16[208,2560]{1,0:T(8,128)(2,1)S(1)}, u32[]{:S(2)}, u32[]{:S(2)}) collective-permute-start(bf16[208,2560]{1,0:T(8,128)(2,1)} %get-tuple-element.18), channel_id=1, source_target_pairs={{0,96},{32,0},{64,32},{96,64},{1,97},{33,1},{65,33},{97,65},{2,98}... | collective-permute-start | bytes 3194888 | tf_op jit(solution)/shard_map/ppermute | solution.py:20
  282.3 50.2 %collective-permute-start.2 = (bf16[208,2560]{1,0:T(8,128)(2,1)}, bf16[208,2560]{1,0:T(8,128)(2,1)S(1)}, u32[]{:S(2)}, u32[]{:S(2)}) collective-permute-start(bf16[208,2560]{1,0:T(8,128)(2,1)} %get-tuple-element.17), channel_id=1, source_target_pairs={{0,32},{32,64},{64,96},{96,0},{1,33},{33,65},{65,97},{97,1},{2,34}... | collective-permute-start | bytes 3194888 | tf_op jit(solution)/shard_map/ppermute | solution.py:20
  335.1 42.1 %copy-start.7 = (f32[128,6]{0,1:T(8,128)S(1)}, f32[128,6]{0,1:T(8,128)}, u32[]{:S(2)}) copy-start(f32[128,6]{0,1:T(8,128)} %param.11) | copy-start | bytes 9220
Sparse Core Ops, SparseCore 0:
  10.2 83.8 all-gather.4
  96.4 81.8 all-gather.2
  219.7 50.6 reduce-scatter.2
  273.4 69.0 reduce-scatter.4
